TPU v7x, 256 devices: a whole 4x4x8 slice. The times are simulated.
256 devices in a mesh: ctx: 32 (over x, y, core), tp: 8 (over z).
Axes of the slice: x: 4, y: 4, z: 8, core: 2. Of those that a mesh axis runs over, the one named last changes fastest.
Arguments:
- tokens: bfloat16 [4096, 4096], P('ctx', 'tp'), may hold values from -6 to 6
- out_grad: bfloat16 [4096, 4096], P('ctx', 'tp'), may hold values from -6 to 6
- route_ids: int32 [4096, 8], P('ctx'), may hold values from 0 to 63, all different within a row; in each aligned block of 128 rows (0 to 127, 128 to 255, ...) at most 24 rows name the same one
- gate_vals: float32 [4096, 8], P('ctx'), may hold values from 0.03 to 0.5
- w_gate_up: bfloat16 [64, 4096, 1536], P('ctx', 'tp'), may hold values from -0.09375 to 0.09375
- w_down: bfloat16 [64, 768, 4096], P('ctx', None, 'tp'), may hold values from -0.21875 to 0.21875
Outputs:
- moe_out: bfloat16 [4096, 4096], P('ctx', 'tp')
- tokens_grad: bfloat16 [4096, 4096], P('ctx', 'tp')
- w_gate_up_grad: bfloat16 [64, 4096, 1536], P('ctx', 'tp')
- w_down_grad: bfloat16 [64, 768, 4096], P('ctx', None, 'tp')
Inputs may be any that keep to these rules, and one draw needn't show every extreme that they name: `route_ids`: each token names 8 different experts. Among the 128 tokens of one index of ctx no expert is named more than 24 times, and in every draw some expert is named exactly 24 times by one such block.
All inputs are finite; a program needn't handle non-finite values.
Results may differ from a plain program's by a relative error of at most 0.0064.
Values may be sent and summed in bfloat16 or wider, within the bound.
A program may use at most 128 MiB of HBM per device.

v0:
```python
import jax
import jax.numpy as jnp
from jax import lax
from jax.sharding import PartitionSpec as P


def activate(gate_up, hidden_width):
    return (jax.nn.silu(gate_up[:, :hidden_width]) * gate_up[:, hidden_width:]).astype(jnp.bfloat16)


def activate_grad(gate_up, hidden_grad, hidden_width):
    gate_part = gate_up[:, :hidden_width]
    up_part = gate_up[:, hidden_width:]
    sigma = jax.nn.sigmoid(gate_part)
    gate_grad = hidden_grad * up_part * sigma * (1.0 + gate_part * (1.0 - sigma))
    up_grad = hidden_grad * jax.nn.silu(gate_part)
    return jnp.concatenate([gate_grad, up_grad], axis=1).astype(jnp.bfloat16)


def rows_product(source, weights, count, per_expert, contract):
    numbers = (((1,), (contract,)), ((), ()))
    owner_rows = jnp.arange(count, dtype=jnp.int32) // per_expert
    accum = None
    for index in range(weights.shape[0]):
        product = lax.dot_general(
            source, weights[index], numbers, preferred_element_type=jnp.float32
        )
        masked = jnp.where((owner_rows == index)[:, None], product, 0.0)
        accum = masked if accum is None else accum + masked
    return accum


def body(tokens, out_grad, route_ids, gate_vals, w_gate_up, w_down):
    n_ctx = lax.axis_size("ctx")
    n_tp = lax.axis_size("tp")
    tok_dev, width_local = tokens.shape
    top_count = route_ids.shape[1]
    exp_dev = w_gate_up.shape[0]
    hidden_width = w_down.shape[1]
    experts = exp_dev * n_ctx
    capacity = 3 * tok_dev * top_count // (2 * experts)
    per_expert = n_ctx * capacity
    total_rows = exp_dev * per_expert
    share_rows = total_rows // n_tp
    flat_routes = route_ids.reshape(-1)
    onehot = (flat_routes[:, None] == jnp.arange(experts, dtype=jnp.int32)[None, :]).astype(
        jnp.int32
    )
    earlier = jnp.cumsum(onehot, axis=0) - onehot
    slot_index = jnp.sum(earlier * onehot, axis=1)
    position = flat_routes * capacity + slot_index
    owner_tokens = jnp.arange(tok_dev * top_count, dtype=jnp.int32) // top_count
    row_table = jnp.full((experts * capacity,), tok_dev, jnp.int32).at[position].set(owner_tokens)
    gate_flat = gate_vals.reshape(-1)
    weight_table = jnp.zeros((experts * capacity,), jnp.float32).at[position].set(gate_flat)
    blank_row = jnp.zeros((1, width_local), jnp.bfloat16)
    send_rows = jnp.concatenate([tokens, blank_row], axis=0)[row_table].reshape(
        experts, capacity, width_local
    )
    picked_grads = jnp.concatenate([out_grad, blank_row], axis=0)[row_table].astype(jnp.float32)
    send_grads = (
        (weight_table[:, None] * picked_grads)
        .astype(jnp.bfloat16)
        .reshape(experts, capacity, width_local)
    )
    rows_in = lax.all_to_all(send_rows, "ctx", split_axis=0, concat_axis=1, tiled=True)
    rows_flat = rows_in.reshape(total_rows, width_local)
    summed = lax.psum_scatter(
        rows_product(rows_flat, w_gate_up, share_rows * lax.axis_size("tp"), per_expert, 0),
        "tp",
        scatter_dimension=0,
        tiled=True,
    )
    hidden = lax.all_gather(activate(summed, hidden_width), "tp", axis=0, tiled=True)
    hidden_cube = hidden.reshape(exp_dev, per_expert, hidden_width)
    expert_out = jnp.einsum(
        "erh,ehd->erd", hidden_cube, w_down, preferred_element_type=jnp.float32
    ).astype(jnp.bfloat16)
    back_out = lax.all_to_all(expert_out, "ctx", split_axis=1, concat_axis=0, tiled=True)
    grads_in = lax.all_to_all(send_grads, "ctx", split_axis=0, concat_axis=1, tiled=True)
    grads_flat = grads_in.reshape(total_rows, width_local)
    hidden_part = lax.psum_scatter(
        rows_product(grads_flat, w_down, share_rows * lax.axis_size("tp"), per_expert, 1),
        "tp",
        scatter_dimension=0,
        tiled=True,
    )
    gate_up_grad = lax.all_gather(
        activate_grad(summed, hidden_part, hidden_width), "tp", axis=0, tiled=True
    )
    grad_cube = gate_up_grad.reshape(exp_dev, per_expert, 2 * hidden_width)
    input_rows = jnp.einsum(
        "erf,edf->erd", grad_cube, w_gate_up, preferred_element_type=jnp.float32
    ).astype(jnp.bfloat16)
    w_gate_up_grad = jnp.einsum(
        "erd,erf->edf", rows_in, grad_cube, preferred_element_type=jnp.float32
    ).astype(jnp.bfloat16)
    w_down_grad = jnp.einsum(
        "erh,erd->ehd", hidden_cube, grads_in, preferred_element_type=jnp.float32
    ).astype(jnp.bfloat16)
    back_grads = lax.all_to_all(input_rows, "ctx", split_axis=1, concat_axis=0, tiled=True)
    out_rows = back_out.reshape(experts * capacity, width_local)[position].astype(jnp.float32)
    moe_out = (out_rows * gate_flat[:, None]).reshape(tok_dev, top_count, width_local).sum(axis=1)
    grad_rows = back_grads.reshape(experts * capacity, width_local)[position].astype(jnp.float32)
    tokens_grad = grad_rows.reshape(tok_dev, top_count, width_local).sum(axis=1)
    return (
        moe_out.astype(jnp.bfloat16),
        tokens_grad.astype(jnp.bfloat16),
        w_gate_up_grad,
        w_down_grad,
    )


def solution(mesh):
    return jax.shard_map(
        body,
        mesh=mesh,
        in_specs=(
            P("ctx", "tp"),
            P("ctx", "tp"),
            P("ctx", None),
            P("ctx", None),
            P("ctx", "tp", None),
            P("ctx", None, "tp"),
        ),
        out_specs=(P("ctx", "tp"), P("ctx", "tp"), P("ctx", "tp", None), P("ctx", None, "tp")),
        check_vma=False,
    )
```

profile of v0, /device:TPU:1, one launch (start us, length us, event | category | flops | bytes accessed | tf_op | source)
XLA Modules:
  0.0 403.5 jit_solution(8359938939187053929)
XLA Ops:
  7.2 0.0 copy-start.2
  7.2 0.7 broadcast_multiply_fusion
  7.9 0.8 copy.44
  8.7 0.1 eq.50
  8.8 0.1 eq.46
  8.9 0.1 copy.43
  9.0 0.1 mul.64
  9.1 0.8 copy.51
  9.9 0.1 reshape.176
  10.0 18.0 %reduce-window.6 = s32[64,8,128]{2,1,0:T(8,128)S(1)} reduce-window(s32[64,8,128]{2,1,0:T(8,128)S(1)} %fusion.16, s32[]{:T(128)} %constant.44.clone.1), window={size=1x1x128 pad=0_0x0_0x127_0}, to_apply=%region_0.0 | reduce-window | flops 8323072 | bytes 524292 | tf_op jit(solution)/shard_map/reduce-window
  28.0 0.1 slice.42
  28.1 0.1 copy.46
  28.3 0.1 copy.47
  28.4 0.1 broadcast_add_fusion
  28.6 0.1 fusion.15
  28.6 4.3 %scatter_custom_fusion = s32[1536]{0:T(1024)S(1)} fusion(s32[1024]{0:T(1024)S(1)} %bitcast.89, s32[1024]{0:T(1024)S(1)} %add_select_fusion.1, s32[]{:T(128)} %constant.47.clone.1), kind=kCustom, calls=%fused_computation.59 | custom fusion | bytes 6148 | tf_op jit(solution)/shard_map/scatter | solution.py:53
  33.0 4.3 %scatter_custom_fusion.1 = f32[1536]{0:T(1024)S(1)} fusion(s32[1024]{0:T(1024)S(1)} %bitcast.90, f32[1024]{0:T(1024)S(1)} %reshape.176, f32[]{:T(128)} %constant.53.clone.1), kind=kCustom, calls=%fused_computation.57 | custom fusion | bytes 6148 | tf_op jit(solution)/shard_map/scatter | solution.py:55
  37.3 0.1 mul.70
  37.4 0.0 copy-done.2
  37.4 4.8 %gather_fusion.2 = bf16[1536,512]{1,0:T(8,128)(2,1)S(1)} fusion(bf16[129,512]{1,0:T(8,128)(2,1)S(1)} %concatenate.11, s32[2048]{0:T(1024)S(1)} %pad_clamp_fusion), kind=kCustom, calls=%fused_computation.2 | custom fusion | bytes 3151872 | tf_op jit(solution)/shard_map/gather | solution.py:60
  42.3 1.5 fusion
  43.8 8.6 %all-to-all-start.2 = ((bf16[64,24,512]{2,1,0:T(8,128)(2,1)}), bf16[64,24,512]{2,1,0:T(8,128)(2,1)S(1)}, u32[]{:S(2)}, u32[]{:S(2)}) async-start(bf16[64,24,512]{2,1,0:T(8,128)(2,1)} %fusion), calls=%async_computation.3 | async-start | bytes 3145728 | tf_op jit(solution)/shard_map/all_to_all | solution.py:80
  52.4 0.0 reduce-scatter.5.cloned.1.call-start
  52.5 22.6 %all-to-all-done.2 = bf16[64,24,512]{2,1,0:T(8,128)(2,1)S(1)} async-done(((bf16[64,24,512]{2,1,0:T(8,128)(2,1)}), bf16[64,24,512]{2,1,0:T(8,128)(2,1)S(1)}, u32[]{:S(2)}, u32[]{:S(2)}) %all-to-all-start.2) | async-done | bytes 1572896 | tf_op jit(solution)/shard_map/all_to_all | solution.py:80
  75.1 0.1 copy.53
  75.2 1.3 copy-done
  76.5 1.4 fusion.8
  77.9 3.5 select_add_fusion.1
  81.5 0.0 reduce-scatter.5.cloned.1.call-update
  81.5 0.0 reduce-scatter.3.cloned.1.call-start
  81.6 0.8 copy-done.3
  82.4 4.8 %gather_fusion = bf16[1536,512]{1,0:T(8,128)(2,1)S(1)} fusion(bf16[129,512]{1,0:T(8,128)(2,1)S(1)} %concatenate.10, s32[2048]{0:T(1024)S(1)} %pad_clamp_fusion), kind=kCustom, calls=%fused_computation | custom fusion | bytes 3151872 | tf_op jit(solution)/shard_map/gather | solution.py:57
  87.2 26.5 %all_to_all.66 = bf16[64,24,512]{2,1,0:T(8,128)(2,1)S(1)} all-to-all(bf16[64,24,512]{2,1,0:T(8,128)(2,1)S(1)} %bitcast.84), channel_id=1, replica_groups=mesh['ctx'=32,'tp'=8] {'ctx'}, dimensions={0} | all-to-all | bytes 3145728 | tf_op jit(solution)/shard_map/all_to_all | solution.py:66
  113.7 0.1 copy.48
  113.8 1.8 copy-done.1
  115.7 2.6 fusion.3
  118.3 5.6 %select_add_fusion = f32[1536,1536]{1,0:T(8,128)} fusion(f32[1536,1536]{1,0:T(8,128)S(1)} %fusion.3, bf16[1536,512]{1,0:T(8,128)(2,1)S(1)} %bitcast.80, pred[1536]{0:T(1024)(128)(4,1)S(1)} %get-tuple-element.8, pred[1536]{0:T(1024)(128)(4,1)S(1)} %get-tuple-element.7, bf16[2,512,1536]{2,1,0:T(8,128)(2,1)S(1)} %copy-done.1), kind=kOutput, calls=%fused_computation.6 | convolution fusion | flops 2422996992 | bytes 22024192 | tf_op jit(solution)/shard_map/dot_general | solution.py:25
  123.9 0.0 reduce-scatter.3.cloned.1.call-update
  123.9 0.2 all-gather.3.cloned.1.call-start
  124.1 16.9 %reduce-scatter.5.cloned.1.call-done = f32[192,768]{1,0:T(8,128)} async-done(((f32[1536,768]{1,0:T(8,128)}), f32[192,768]{1,0:T(8,128)}) %reduce-scatter.5.cloned.1.call-update) | async-done | bytes 589840 | tf_op jit(solution)/shard_map/reduce_scatter | solution.py:82
  141.0 106.0 %reduce-scatter.3.cloned.1.call-done = f32[192,1536]{1,0:T(8,128)} async-done(((f32[1536,1536]{1,0:T(8,128)}), f32[192,1536]{1,0:T(8,128)}) %reduce-scatter.3.cloned.1.call-update) | async-done | bytes 1179664 | tf_op jit(solution)/shard_map/reduce_scatter | solution.py:68
  247.1 2.6 multiply_convert_fusion.1
  249.6 0.0 all-gather.3.cloned.1.call-update
  249.7 0.0 all-gather.5.cloned.1.call-start
  249.7 1.8 pad_maximum_fusion
  251.5 0.0 all-gather.5.cloned.1.call-update
  251.6 35.5 %all-gather.3.cloned.1.call-done = bf16[1536,768]{1,0:T(8,128)(2,1)} async-done(((bf16[192,768]{1,0:T(8,128)(2,1)}), bf16[1536,768]{1,0:T(8,128)(2,1)}) %all-gather.3.cloned.1.call-update) | async-done | bytes 2359312 | tf_op jit(solution)/shard_map/all_gather | solution.py:74
  287.1 3.5 convolution_convert_fusion.2
  290.6 2.8 copy.49
  293.4 10.5 %all-to-all-start.1 = ((bf16[2,768,512]{2,0,1:T(2,128)(2,1)}), bf16[2,768,512]{2,0,1:T(2,128)(2,1)}, u32[]{:S(2)}, u32[]{:S(2)}) async-start(bf16[2,768,512]{2,0,1:T(2,128)(2,1)} %copy.49), calls=%async_computation.2 | async-start | bytes 3145728 | tf_op jit(solution)/shard_map/all_to_all | solution.py:79
  303.9 46.9 %all-gather.5.cloned.1.call-done = bf16[1536,1536]{1,0:T(8,128)(2,1)} async-done(((bf16[192,1536]{1,0:T(8,128)(2,1)}), bf16[1536,1536]{1,0:T(8,128)(2,1)}) %all-gather.5.cloned.1.call-update) | async-done | bytes 4718608 | tf_op jit(solution)/shard_map/all_gather | solution.py:88
  350.8 6.0 %convolution_convert_fusion.3 = bf16[2,768,512]{2,1,0:T(8,128)(2,1)S(1)} fusion(bf16[2,768,1536]{2,1,0:T(8,128)(2,1)} %bitcast.92, bf16[2,512,1536]{2,1,0:T(8,128)(2,1)} %param.10), kind=kOutput, calls=%fused_computation.15 | convolution fusion | flops 2416705536 | bytes 9437184 | tf_op jit(solution)/shard_map/erf,edf->erd/dot_general | solution.py:92
  356.7 2.8 copy.54
  359.6 0.0 all-to-all-done.1
  359.6 7.6 %all-to-all-start.3 = ((bf16[2,768,512]{2,0,1:T(2,128)(2,1)}), bf16[2,768,512]{2,0,1:T(2,128)(2,1)}, u32[]{:S(2)}, u32[]{:S(2)}) async-start(bf16[2,768,512]{2,0,1:T(2,128)(2,1)} %copy.54), calls=%async_computation.5 | async-start | bytes 3145728 | tf_op jit(solution)/shard_map/all_to_all | solution.py:101
  367.2 4.2 %convolution_convert_fusion.1 = bf16[2,768,512]{2,1,0:T(8,128)(2,1)} fusion(bf16[2,768,768]{2,1,0:T(8,128)(2,1)} %bitcast.95, bf16[2,768,512]{2,1,0:T(8,128)(2,1)S(1)} %bitcast.78), kind=kOutput, calls=%fused_computation.13 | convolution fusion | flops 1208745984 | bytes 5505024 | tf_op jit(solution)/shard_map/erh,erd->ehd/dot_general | solution.py:98
  371.4 1.7 copy.50
  373.2 5.1 %gather_fusion.1 = bf16[1024,512]{1,0:T(8,128)(2,1)} fusion(bf16[1536,512]{1,0:T(8,128)(2,1)S(1)} %bitcast.75, s32[1024]{0:T(1024)S(1)} %broadcast_clamp_fusion), kind=kCustom, calls=%fused_computation.1 | custom fusion | bytes 2101248 | tf_op jit(solution)/shard_map/gather | solution.py:102
  378.2 2.6 fusion.1
  380.8 6.4 %convolution_convert_fusion = bf16[2,512,1536]{2,1,0:T(8,128)(2,1)} fusion(bf16[2,768,512]{2,1,0:T(8,128)(2,1)S(1)} %bitcast.81, bf16[2,768,1536]{2,1,0:T(8,128)(2,1)} %bitcast.93), kind=kOutput, calls=%fused_computation.8 | convolution fusion | flops 2417491968 | bytes 9437184 | tf_op jit(solution)/shard_map/erd,erf->edf/dot_general | solution.py:95
  387.2 2.7 all-to-all-done.3
  389.9 1.7 copy.55
  391.6 4.0 gather_fusion.3
  395.6 1.3 bitcast_reduce_fusion
  (14 shorter events, 0.1 us)
Async XLA Ops:
  7.2 30.2 %copy-start.2 = (bf16[128,512]{1,0:T(8,128)(2,1)S(1)}, bf16[128,512]{1,0:T(8,128)(2,1)}, u32[]{:S(2)}) copy-start(bf16[128,512]{1,0:T(8,128)(2,1)} %param.7) | copy-start | bytes 393220
  43.8 31.3 %all-to-all-start.2 = ((bf16[64,24,512]{2,1,0:T(8,128)(2,1)}), bf16[64,24,512]{2,1,0:T(8,128)(2,1)S(1)}, u32[]{:S(2)}, u32[]{:S(2)}) async-start(bf16[64,24,512]{2,1,0:T(8,128)(2,1)} %fusion), calls=%async_computation.3 | async-start | bytes 3145728 | tf_op jit(solution)/shard_map/all_to_all | solution.py:80
  52.4 88.6 %reduce-scatter.5.cloned.1.call-start = ((), (), s32[]{:S(2)}) async-start(), calls=%async_computation.8 | async-start | bytes 5308416 | tf_op jit(solution)/shard_map/reduce_scatter | solution.py:82
  75.1 1.4 copy-start
  81.5 0.9 copy-start.3
  81.5 165.6 %reduce-scatter.3.cloned.1.call-start = ((), (), s32[]{:S(2)}) async-start(), calls=%async_computation.6 | async-start | bytes 10616832 | tf_op jit(solution)/shard_map/reduce_scatter | solution.py:68
  113.7 1.9 copy-start.1
  123.9 163.2 %all-gather.3.cloned.1.call-start = ((), (), s32[]{:S(2)}) async-start(), calls=%async_computation.7 | async-start | bytes 2654208 | tf_op jit(solution)/shard_map/all_gather | solution.py:74
  249.7 101.1 %all-gather.5.cloned.1.call-start = ((), (), s32[]{:S(2)}) async-start(), calls=%async_computation.9 | async-start | bytes 5308416 | tf_op jit(solution)/shard_map/all_gather | solution.py:88
  293.4 66.2 %all-to-all-start.1 = ((bf16[2,768,512]{2,0,1:T(2,128)(2,1)}), bf16[2,768,512]{2,0,1:T(2,128)(2,1)}, u32[]{:S(2)}, u32[]{:S(2)}) async-start(bf16[2,768,512]{2,0,1:T(2,128)(2,1)} %copy.49), calls=%async_computation.2 | async-start | bytes 3145728 | tf_op jit(solution)/shard_map/all_to_all | solution.py:79
  359.6 30.3 %all-to-all-start.3 = ((bf16[2,768,512]{2,0,1:T(2,128)(2,1)}), bf16[2,768,512]{2,0,1:T(2,128)(2,1)}, u32[]{:S(2)}, u32[]{:S(2)}) async-start(bf16[2,768,512]{2,0,1:T(2,128)(2,1)} %copy.54), calls=%async_computation.5 | async-start | bytes 3145728 | tf_op jit(solution)/shard_map/all_to_all | solution.py:101
Sparse Core Ops, SparseCore 0:
  81.6 59.3 reduce-scatter.4
  143.6 103.4 reduce-scatter.2
  249.8 37.2 all-gather.2
  289.3 61.4 all-gather.4
where the time goes:
time: 404 us; the launch traced here: 403 us
  waiting for transfers between devices  231 us (57%)
  local copies, waits for them, and re-layouts  43 us (11%)
  matrix products  33.2 us (8%)
  other arithmetic  28.9 us (7%)
  starting transfers between devices  27 us (7%)
  blocking collectives  26.5 us (7%)
  between operations  14 us (3%)
    reduce_scatter x1, waiting for transfers between devices, body(): lax.psum_scatter(rows_product(rows_flat, w_gate_up, share_rows * lax.axis...  106 us
    all_gather x1, waiting for transfers between devices, body(): lax.all_gather(activate_grad(summed, hidden_part, hidden_width), 'tp', ax...  46.9 us
    all_gather x1, waiting for transfers between devices, body(): lax.all_gather(activate(summed, hidden_width), 'tp', axis=0, tiled=True)  35.5 us
    all_to_all x1, blocking collectives, body(): lax.all_to_all(send_rows, 'ctx', split_axis=0, concat_axis=1, tiled=True)  26.5 us
    all_to_all x1, waiting for transfers between devices, body(): lax.all_to_all(send_grads, 'ctx', split_axis=0, concat_axis=1, tiled=True)  22.6 us
    another operation x4, other arithmetic  20.8 us
    reduce_scatter x1, waiting for transfers between devices, body(): lax.psum_scatter(rows_product(grads_flat, w_down, share_rows * lax.axis_s...  16.9 us
    dot_general x4, matrix products, rows_product(): lax.dot_general(source, weights[index], numbers, preferred_element_type=j...  13.2 us
  transfers between devices with their start and end apart: 7, of which 6 were waited for; matrix products, arithmetic and copies ran while one was open for 12% of the time, Pallas kernels for 0%

commit v1 on v0

v1 whole, which is shorter than its diff:
```python
import functools

import jax
import jax.numpy as jnp
from jax import lax
from jax.experimental import pallas as pl
from jax.experimental.pallas import tpu as pltpu
from jax.sharding import PartitionSpec as P

BF = jnp.bfloat16
F32 = jnp.float32
MESH = pl.DeviceIdType.MESH
SIDE = 4
CORES = 2
CHUNKS = 4
SPOTS = 8
RING = 8

OFFSETS = (
    ((0, 0), (1, 0), (3, 0), (0, 1)),
    ((2, 0), (0, 2), (1, 3), (2, 1)),
    ((2, 2), (1, 2), (3, 2), (2, 3)),
    ((0, 3), (1, 1), (3, 3), (3, 1)),
)


def dot(a, b, ca=1, cb=0):
    return lax.dot_general(a, b, (((ca,), (cb,)), ((), ())), preferred_element_type=F32)


def pick(chunk, values):
    result = values[-1]
    for index in range(len(values) - 2, -1, -1):
        result = jnp.where(chunk == index, values[index], result)
    return result


def kernel(
    tokens, out_grad, routes, gates, w_gu, w_dn,
    moe_out, tokens_grad, wgu_out, wdn_out,
    tg, pick_all, gate_all, pick_c, gate_hi, gate_lo,
    x_send, x_recv, rows, wgu, wdn, part, rs_send, rs_recv, act, fin, r_recv, wgu_st, wdn_st,
    ld_sem, xs_sem, xr_sem, rss_sem, rsr_sem, ags_sem, agr_sem, rts_sem, rtr_sem, out_sem,
):
    ctx = lax.axis_index("ctx")
    tp = lax.axis_index("tp")
    n_ctx = SIDE * SIDE * CORES
    core = lax.rem(ctx, CORES)
    my_y = lax.rem(ctx // CORES, SIDE)
    my_x = ctx // (CORES * SIDE)
    up = lax.rem(tp + 1, RING)
    down = lax.rem(tp + RING - 1, RING)
    tok, top = routes.shape
    width = tokens.shape[1]
    ff = wdn.shape[1]
    cap = x_send.shape[2] // 2
    block = 2 * cap
    exp_rows = n_ctx * cap
    half_rows = SPOTS * cap
    half = 3 * ff // 2
    strip = ff // 2
    experts = 2 * n_ctx

    barrier = pltpu.get_barrier_semaphore()

    def greet(i, carry):
        pl.semaphore_signal(
            barrier, inc=1, device_id=(lax.rem(ctx + 1 + i, n_ctx), tp), device_id_type=MESH
        )
        return carry

    lax.fori_loop(0, n_ctx - 1, greet, 0)
    pl.semaphore_signal(barrier, inc=1, device_id=(ctx, up), device_id_type=MESH)
    pl.semaphore_signal(barrier, inc=1, device_id=(ctx, down), device_id_type=MESH)

    loads = [
        pltpu.make_async_copy(tokens, tg.at[:, pl.ds(0, width)], ld_sem.at[0]),
        pltpu.make_async_copy(out_grad, tg.at[:, pl.ds(width, width)], ld_sem.at[1]),
        pltpu.make_async_copy(w_gu, wgu, ld_sem.at[2]),
        pltpu.make_async_copy(w_dn, wdn, ld_sem.at[3]),
    ]
    for load in loads:
        load.start()

    lanes = lax.broadcasted_iota(jnp.int32, (tok, 128), 1)
    named = jnp.zeros((tok, 128), F32)
    gate_of = jnp.zeros((tok, 128), F32)
    for k in range(top):
        hit = routes[:, k : k + 1] == lanes
        named = named + jnp.where(hit, 1.0, 0.0)
        gate_of = gate_of + jnp.where(hit, gates[:, k : k + 1], 0.0)
    named_t = named.T
    gate_t = gate_of.T[:experts]
    before = (
        lax.broadcasted_iota(jnp.int32, (tok, tok), 0)
        < lax.broadcasted_iota(jnp.int32, (tok, tok), 1)
    )
    earlier = dot(named_t.astype(BF), jnp.where(before, 1.0, 0.0).astype(BF))[:experts]
    slot = jnp.where(named_t[:experts] > 0.5, earlier, -1.0)
    group = 8
    for g in range(experts // group):
        part_slot = slot[g * group : (g + 1) * group][:, None, :]
        part_gate = gate_t[g * group : (g + 1) * group][:, None, :]
        wanted = lax.broadcasted_iota(jnp.int32, (group, cap, tok), 1).astype(F32)
        owned = part_slot == wanted
        span = pl.ds(g * group * cap, group * cap)
        pick_all[span, :] = jnp.where(owned, 1.0, 0.0).reshape(group * cap, tok).astype(BF)
        gate_all[span, :] = jnp.where(owned, part_gate, 0.0).reshape(group * cap, tok)
    loads[0].wait()
    loads[1].wait()

    def peer(chunk, q, sign):
        dx = pick(chunk, [OFFSETS[c][q][0] for c in range(CHUNKS)])
        dy = pick(chunk, [OFFSETS[c][q][1] for c in range(CHUNKS)])
        px = lax.rem(my_x + sign * dx + SIDE, SIDE)
        py = lax.rem(my_y + sign * dy + SIDE, SIDE)
        return (px * SIDE + py) * CORES

    def dispatch(chunk, i):
        q, b = i // 2, i % 2
        return pltpu.make_async_remote_copy(
            src_ref=x_send.at[chunk, i], dst_ref=x_recv.at[chunk, 2 * q + core],
            send_sem=xs_sem.at[chunk, i], recv_sem=xr_sem.at[chunk, 2 * q + core],
            device_id=(peer(chunk, q, -1) + b, tp), device_id_type=MESH,
        )

    def arrival(chunk, i):
        return pltpu.make_async_remote_copy(
            src_ref=x_send.at[chunk, i], dst_ref=x_recv.at[chunk, i],
            send_sem=xs_sem.at[chunk, i], recv_sem=xr_sem.at[chunk, i],
            device_id=(peer(chunk, i // 2, 1) + i % 2, tp), device_id_type=MESH,
        )

    def back(chunk, i):
        q, b = i // 2, i % 2
        return pltpu.make_async_remote_copy(
            src_ref=x_send.at[chunk, i], dst_ref=r_recv.at[chunk, 2 * q + core],
            send_sem=rts_sem.at[chunk, i], recv_sem=rtr_sem.at[chunk, 2 * q + core],
            device_id=(peer(chunk, q, 1) + b, tp), device_id_type=MESH,
        )

    def back_arrival(chunk, i):
        return pltpu.make_async_remote_copy(
            src_ref=x_send.at[chunk, i], dst_ref=r_recv.at[chunk, i],
            send_sem=rts_sem.at[chunk, i], recv_sem=rtr_sem.at[chunk, i],
            device_id=(peer(chunk, i // 2, -1) + i % 2, tp), device_id_type=MESH,
        )

    def remote_only(chunk, i, act_on):
        if i < 2:
            pl.when(jnp.logical_or(chunk != 0, core != i))(act_on)
        else:
            act_on()

    def build(chunk):
        for i in range(SPOTS):
            dest = peer(chunk, i // 2, -1) + i % 2
            span = pl.ds(pl.multiple_of(dest * block, block), block)
            here = pl.ds(i * block, block)
            pick_c[chunk, here, :] = pick_all[span, :]
            weights = gate_all[span, :]
            high = weights.astype(BF)
            gate_hi[chunk, here, :] = high
            gate_lo[chunk, here, :] = (weights - high.astype(F32)).astype(BF)
            fin[pl.ds(i * block, block), 0:1] = jnp.sum(weights, axis=1, keepdims=True)
        chosen = dot(pick_c[chunk], tg[:, 0:width])
        x_send[chunk, :, :, 0:width] = chosen.astype(BF).reshape(SPOTS, block, width)
        chosen = dot(pick_c[chunk], tg[:, width : 2 * width]) * fin[:, 0:1]
        x_send[chunk, :, :, width : 2 * width] = chosen.astype(BF).reshape(SPOTS, block, width)

    def send_rows(chunk):
        for i in range(SPOTS):
            remote_only(chunk, i, lambda i=i: dispatch(chunk, i).start())

    def take_rows(chunk):
        for i in range(SPOTS):
            remote_only(chunk, i, lambda i=i: arrival(chunk, i).wait_recv())
        for pair in range(SPOTS // 2):
            first = x_recv[chunk, 2 * pair].astype(F32)
            second = x_recv[chunk, 2 * pair + 1].astype(F32)
            for e in range(2):
                both = jnp.concatenate(
                    [first[e * cap : (e + 1) * cap], second[e * cap : (e + 1) * cap]], axis=0
                )
                start = e * exp_rows + chunk * half_rows + pair * block
                rows[pl.ds(pl.multiple_of(start, 16), block), :] = both.astype(BF)

    def products(chunk):
        side = lax.rem(chunk, 2)
        for e in range(2):
            span = pl.ds(pl.multiple_of(e * exp_rows + chunk * half_rows, 16), half_rows)
            out = pl.ds(e * half_rows, half_rows)
            left = rows[span, 0:width]
            for n in range(4):
                cols = slice(n * strip, (n + 1) * strip)
                part[side, out, cols] = dot(left, wgu[e, :, cols])
            left = rows[span, width : 2 * width]
            for n in range(2):
                part[side, out, (4 + n) * strip : (5 + n) * strip] = dot(
                    left, wdn[e, n * strip : (n + 1) * strip, :], 1, 1
                )

    def own_rows(owner):
        return pl.ds(pl.multiple_of(owner * block, block), block)

    def rs_copy(chunk, way, step):
        side = lax.rem(chunk, 2)
        src, dst = rs_send.at[side, way, step], rs_recv.at[chunk, way, step]
        if step == 0:
            src, dst = src.at[way], dst.at[way]
        return pltpu.make_async_remote_copy(
            src_ref=src, dst_ref=dst,
            send_sem=rss_sem.at[chunk, way, step], recv_sem=rsr_sem.at[chunk, way, step],
            device_id=(ctx, (up, down)[way]), device_id_type=MESH,
        )

    def rs_drain(chunk):
        for way in range(2):
            for step in range(4):
                rs_copy(chunk, way, step).wait_send()

    def rs_first(chunk):
        side = lax.rem(chunk, 2)
        pl.when(chunk >= 2)(lambda: rs_drain(chunk - 2))
        owner = lax.rem(tp + 4, RING)
        for way in range(2):
            rs_send[side, way, 0, way] = part[
                side, own_rows(owner), way * half : (way + 1) * half
            ].astype(BF)
            rs_copy(chunk, way, 0).start()

    def rs_step(chunk, step):
        side = lax.rem(chunk, 2)
        for way in range(2):
            owner = lax.rem(tp + (4 - step if way == 0 else 4 + step), RING)
            rs_copy(chunk, way, step - 1).wait_recv()
            for h in range(2):
                value = part[side, own_rows(owner), h * half : (h + 1) * half]
                if step > 1 or h == way:
                    value = value + rs_recv[chunk, way, step - 1, h].astype(F32)
                rs_send[side, way, step, h] = value.astype(BF)
            rs_copy(chunk, way, step).start()

    def act_rows(chunk, owner):
        start = (owner // 4) * exp_rows + chunk * half_rows + lax.rem(owner, 4) * block
        return pl.ds(pl.multiple_of(start, 16), block)

    def rs_last(chunk):
        side = lax.rem(chunk, 2)
        for way in range(2):
            rs_copy(chunk, way, 3).wait_recv()

        def total(s):
            h, at = s // 3, (s % 3) * strip
            value = part[side, own_rows(tp), s * strip : (s + 1) * strip]
            for way in range(2):
                value = value + rs_recv[chunk, way, 3, h, :, at : at + strip].astype(F32)
            return value

        out = act_rows(chunk, tp)
        for t in range(2):
            gate, upper, grad = total(t), total(2 + t), total(4 + t)
            sigma = jax.nn.sigmoid(gate)
            silu = gate * sigma
            act[out, t * strip : (t + 1) * strip] = (silu * upper).astype(BF)
            act[out, (2 + t) * strip : (3 + t) * strip] = (
                grad * upper * sigma * (1.0 + gate * (1.0 - sigma))
            ).astype(BF)
            act[out, (4 + t) * strip : (5 + t) * strip] = (grad * silu).astype(BF)

    def ag_copy(chunk, way, step):
        owner = lax.rem(tp + (RING - step if way == 0 else step), RING)
        span = act_rows(chunk, owner)
        ref = act.at[span, :] if step < 3 else act.at[span, pl.ds(way * half, half)]
        return pltpu.make_async_remote_copy(
            src_ref=ref, dst_ref=ref,
            send_sem=ags_sem.at[chunk, way, step], recv_sem=agr_sem.at[chunk, way, step],
            device_id=(ctx, (up, down)[way]), device_id_type=MESH,
        )

    def ag_arrival(chunk, way, step):
        owner = lax.rem(tp + (2 * RING - step - 1 if way == 0 else step + 1), RING)
        span = act_rows(chunk, owner)
        ref = act.at[span, :] if step < 3 else act.at[span, pl.ds(way * half, half)]
        return pltpu.make_async_remote_copy(
            src_ref=ref, dst_ref=ref,
            send_sem=ags_sem.at[chunk, way, step], recv_sem=agr_sem.at[chunk, way, step],
            device_id=(ctx, (up, down)[way]), device_id_type=MESH,
        )

    def ag_step(chunk, step):
        for way in range(2):
            if step > 0:
                ag_arrival(chunk, way, step - 1).wait_recv()
            ag_copy(chunk, way, step).start()

    def ag_last(chunk):
        for way in range(2):
            ag_arrival(chunk, way, 3).wait_recv()

    def finish(chunk):
        for i in range(SPOTS):
            remote_only(chunk, i, lambda i=i: dispatch(chunk, i).wait_send())
        for e in range(2):
            span = pl.ds(pl.multiple_of(e * exp_rows + chunk * half_rows, 16), half_rows)
            out = pl.ds(e * half_rows, half_rows)
            fin[out, 0:width] = dot(act[span, 0:ff], wdn[e])
            fin[out, width : 2 * width] = dot(act[span, ff : 3 * ff], wgu[e], 1, 1)
        for i in range(SPOTS):
            both = jnp.concatenate(
                [
                    fin[i * cap : (i + 1) * cap, :],
                    fin[half_rows + i * cap : half_rows + (i + 1) * cap, :],
                ],
                axis=0,
            )
            x_send[chunk, i] = both.astype(BF)
            remote_only(chunk, i, lambda i=i: back(chunk, i).start())

    build(0)
    pl.semaphore_wait(barrier, n_ctx + 1)
    send_rows(0)
    x_recv[0, core] = x_send[0, core]
    build(1)
    loads[2].wait()
    loads[3].wait()
    take_rows(0)
    products(0)
    rs_first(0)
    send_rows(1)

    def phase(i, carry):
        summing = i < CHUNKS
        gathering = i >= 1

        @pl.when(i + 2 < CHUNKS)
        def _():
            build(i + 2)
            send_rows(i + 2)

        pl.when(gathering)(lambda: ag_step(i - 1, 1))
        pl.when(summing)(lambda: rs_step(i, 1))

        @pl.when(i + 1 < CHUNKS)
        def _():
            take_rows(i + 1)
            products(i + 1)
            rs_first(i + 1)

        pl.when(gathering)(lambda: ag_step(i - 1, 2))
        pl.when(summing)(lambda: rs_step(i, 2))
        pl.when(i >= 2)(lambda: finish(i - 2))
        pl.when(gathering)(lambda: ag_step(i - 1, 3))
        pl.when(summing)(lambda: rs_step(i, 3))

        @pl.when(summing)
        def _():
            rs_last(i)
            ag_step(i, 0)

        pl.when(gathering)(lambda: ag_last(i - 1))
        return carry

    lax.fori_loop(0, CHUNKS + 1, phase, 0)
    finish(CHUNKS - 1)
    r_recv[0, core] = x_send[0, core]

    stores = []
    for e in range(2):
        span = slice(e * exp_rows, (e + 1) * exp_rows)
        for n in range(2):
            cols = slice(n * ff, (n + 1) * ff)
            wgu_st[e, :, cols] = dot(
                rows[span, 0:width], act[span, (1 + n) * ff : (2 + n) * ff], 0, 0
            ).astype(BF)
        stores.append(pltpu.make_async_copy(wgu_st.at[e], wgu_out.at[e], out_sem.at[e]))
        stores[-1].start()
        wdn_st[e] = dot(act[span, 0:ff], rows[span, width : 2 * width], 0, 0).astype(BF)
        stores.append(pltpu.make_async_copy(wdn_st.at[e], wdn_out.at[e], out_sem.at[2 + e]))
        stores[-1].start()

    out_sum = jnp.zeros((tok, width), F32)
    in_sum = jnp.zeros((tok, width), F32)
    for chunk in range(CHUNKS):
        for i in range(SPOTS):
            remote_only(chunk, i, lambda i=i, chunk=chunk: back_arrival(chunk, i).wait_recv())
        came = r_recv[chunk, :, :, 0:width].reshape(SPOTS * block, width)
        out_sum = out_sum + dot(gate_hi[chunk], came, 0, 0) + dot(gate_lo[chunk], came, 0, 0)
        came = r_recv[chunk, :, :, width : 2 * width].reshape(SPOTS * block, width)
        in_sum = in_sum + dot(pick_c[chunk], came, 0, 0)
    moe_out[...] = out_sum.astype(BF)
    tokens_grad[...] = in_sum.astype(BF)

    for chunk in range(CHUNKS):
        for way in range(2):
            for step in range(4):
                ag_copy(chunk, way, step).wait_send()
        for i in range(SPOTS):
            remote_only(chunk, i, lambda i=i, chunk=chunk: back(chunk, i).wait_send())
    rs_drain(CHUNKS - 2)
    rs_drain(CHUNKS - 1)
    for store in stores:
        store.wait()


def body(tokens, out_grad, routes, gates, w_gu, w_dn):
    tok, width = tokens.shape
    top = routes.shape[1]
    ff = w_dn.shape[1]
    n_ctx = SIDE * SIDE * CORES
    cap = 3 * tok * top // (4 * n_ctx)
    block = 2 * cap
    chunk_rows = SPOTS * block
    all_rows = CHUNKS * chunk_rows
    half = 3 * ff // 2
    dma = pltpu.SemaphoreType.DMA
    any_space = pl.BlockSpec(memory_space=pl.ANY)
    vmem = pl.BlockSpec(memory_space=pltpu.VMEM)
    flops = 6 * all_rows * width * 3 * ff
    return pl.pallas_call(
        kernel,
        out_shape=(
            jax.ShapeDtypeStruct((tok, width), BF),
            jax.ShapeDtypeStruct((tok, width), BF),
            jax.ShapeDtypeStruct(w_gu.shape, BF),
            jax.ShapeDtypeStruct(w_dn.shape, BF),
        ),
        in_specs=[any_space, any_space, vmem, vmem, any_space, any_space],
        out_specs=(vmem, vmem, any_space, any_space),
        scratch_shapes=[
            pltpu.VMEM((tok, 2 * width), BF),
            pltpu.VMEM((all_rows, tok), BF),
            pltpu.VMEM((all_rows, tok), F32),
            pltpu.VMEM((CHUNKS, chunk_rows, tok), BF),
            pltpu.VMEM((CHUNKS, chunk_rows, tok), BF),
            pltpu.VMEM((CHUNKS, chunk_rows, tok), BF),
            pltpu.VMEM((CHUNKS, SPOTS, block, 2 * width), BF),
            pltpu.VMEM((CHUNKS, SPOTS, block, 2 * width), BF),
            pltpu.VMEM((all_rows, 2 * width), BF),
            pltpu.VMEM(w_gu.shape, BF),
            pltpu.VMEM(w_dn.shape, BF),
            pltpu.VMEM((2, chunk_rows, 3 * ff), F32),
            pltpu.VMEM((2, 2, 4, 2, block, half), BF),
            pltpu.VMEM((CHUNKS, 2, 4, 2, block, half), BF),
            pltpu.VMEM((all_rows, 3 * ff), BF),
            pltpu.VMEM((chunk_rows, 2 * width), F32),
            pltpu.VMEM((CHUNKS, SPOTS, block, 2 * width), BF),
            pltpu.VMEM(w_gu.shape, BF),
            pltpu.VMEM(w_dn.shape, BF),
            dma((4,)),
            dma((CHUNKS, SPOTS)),
            dma((CHUNKS, SPOTS)),
            dma((CHUNKS, 2, 4)),
            dma((CHUNKS, 2, 4)),
            dma((CHUNKS, 2, 4)),
            dma((CHUNKS, 2, 4)),
            dma((CHUNKS, SPOTS)),
            dma((CHUNKS, SPOTS)),
            dma((4,)),
        ],
        compiler_params=pltpu.CompilerParams(
            collective_id=0, has_side_effects=True, vmem_limit_bytes=60 * 1024 * 1024
        ),
        cost_estimate=pl.CostEstimate(flops=flops, bytes_accessed=10 << 20, transcendentals=0),
        name="moe",
    )(tokens, out_grad, routes, gates, w_gu, w_dn)


def solution(mesh):
    return jax.shard_map(
        body,
        mesh=mesh,
        in_specs=(
            P("ctx", "tp"),
            P("ctx", "tp"),
            P("ctx", None),
            P("ctx", None),
            P("ctx", "tp", None),
            P("ctx", None, "tp"),
        ),
        out_specs=(P("ctx", "tp"), P("ctx", "tp"), P("ctx", "tp", None), P("ctx", None, "tp")),
        check_vma=False,
    )
```

time: 404 us -> 213 us (0.53)
  waiting for transfers between devices: 231 us -> 0 us
  Pallas kernels: 0 us -> 201 us
  matrix products: 33.2 us -> 0 us
  local copies, waits for them, and re-layouts: 43 us -> 11 us
  other arithmetic: 28.9 us -> 0 us
  starting transfers between devices: 27 us -> 0 us
  blocking collectives: 26.5 us -> 0 us
  between operations: 14 us -> 0.64 us
    pallas_call x0 -> x1, Pallas kernels: none -> 201 us  [body(): pl.pallas_call(kernel, out_shape=(jax.ShapeDtypeStruct((tok, width), BF),...]
    reduce_scatter x2 -> x0, waiting for transfers between devices: 123 us -> none  [the longest x1 106 us: body(): lax.psum_scatter(rows_product(rows_flat, w_gate_up, share_rows * lax.axis...]
    all_gather x2 -> x0, waiting for transfers between devices: 82.4 us -> none  [the longest x1 46.9 us: body(): lax.all_gather(activate_grad(summed, hidden_part, hidden_width), 'tp', ax...]
    dot_general x8 -> x0, matrix products: 33.2 us -> none  [the longest x4 13.2 us: rows_product(): lax.dot_general(source, weights[index], numbers, preferred_element_type=j...]
    all_to_all x3 -> x0, starting transfers between devices: 26.7 us -> none  [the longest x1 10.5 us: body(): lax.all_to_all(expert_out, 'ctx', split_axis=1, concat_axis=0, tiled=True)]
    all_to_all x1 -> x0, blocking collectives: 26.5 us -> none  [body(): lax.all_to_all(send_rows, 'ctx', split_axis=0, concat_axis=1, tiled=True)]
    all_to_all x3 -> x0, waiting for transfers between devices: 25.3 us -> none  [the longest x1 22.6 us: body(): lax.all_to_all(send_grads, 'ctx', split_axis=0, concat_axis=1, tiled=True)]
    another operation x4 -> x0, other arithmetic: 20.8 us -> none
  transfers between devices with their start and end apart: 7 -> 0, of which waited for: 6 -> 0; matrix products, arithmetic and copies ran while one was open for 12% -> 0% of each run, Pallas kernels for 0% -> 0%
where the time goes in v1:
time: 213 us; the launch traced here: 212 us
  Pallas kernels  201 us (94%)
  local copies, waits for them, and re-layouts  11 us (5%)
    pallas_call x1, Pallas kernels, body(): pl.pallas_call(kernel, out_shape=(jax.ShapeDtypeStruct((tok, width), BF),...  201 us
    unnamed x8, local copies, waits for them, and re-layouts  11 us

profile of v1, /device:TPU:1, one launch (start us, length us, event | category | flops | bytes accessed | tf_op | source)
XLA Modules:
  0.0 212.3 jit_solution(6788321782346646236)
XLA Ops:
  0.6 1.4 copy.10.routes
  2.0 1.4 copy.11.gates
  3.5 200.6 %moe.1 = (bf16[128,512]{1,0:T(8,128)(2,1)}, bf16[128,512]{1,0:T(8,128)(2,1)}, bf16[2,512,1536]{2,1,0:T(8,128)(2,1)}, bf16[2,768,512]{2,1,0:T(8,128)(2,1)}) custom-call(bf16[128,512]{1,0:T(8,128)(2,1)} %tokens.1, bf16[128,512]{1,0:T(8,128)(2,1)} %out_grad.1, s32[128,8]{1,0:T(8,128)} %copy.10.routes, f32[128,8]{1,0:T(8,128)} %copy.11.gates, ...), custom_call_target="tpu_custom_call" | custom-call | flops 10871635968 | bytes 10485760 | tf_op jit(solution)/shard_map/moe/pallas_call | solution.py:420
  204.1 1.6 copy.16
  205.7 1.6 copy.17
  207.2 0.0 copy-start
  207.2 3.9 %copy.18 = bf16[2,512,1536]{2,1,0:T(8,128)(2,1)} copy(bf16[2,512,1536]{2,1,0:T(8,128)(2,1)} %get-tuple-element.10) | data formatting | bytes 6291456
  211.1 0.0 copy-done
  211.1 1.1 copy.19
Async XLA Ops:
  207.2 3.9 %copy-start = (bf16[2,768,512]{2,1,0:T(8,128)(2,1)S(1)}, bf16[2,768,512]{2,1,0:T(8,128)(2,1)}, u32[]{:S(2)}) copy-start(bf16[2,768,512]{2,1,0:T(8,128)(2,1)} %get-tuple-element.11) | copy-start | bytes 4718596

commit v2 on v1

v2 whole, which is shorter than its diff:
```python
import functools

import jax
import jax.numpy as jnp
from jax import lax
from jax.experimental import pallas as pl
from jax.experimental.pallas import tpu as pltpu
from jax.sharding import PartitionSpec as P

BF = jnp.bfloat16
F32 = jnp.float32
MESH = pl.DeviceIdType.MESH
SIDE = 4
CORES = 2
CHUNKS = 4
SPOTS = 8
RING = 8

OFFSETS = (
    ((0, 0), (1, 0), (3, 0), (0, 1)),
    ((2, 0), (0, 2), (2, 2), (3, 3)),
    ((2, 1), (2, 3), (1, 2), (3, 2)),
    ((0, 3), (1, 1), (3, 1), (1, 3)),
)


def dot(a, b, ca=1, cb=0):
    return lax.dot_general(a, b, (((ca,), (cb,)), ((), ())), preferred_element_type=F32)


def pick(chunk, values):
    result = values[-1]
    for index in range(len(values) - 2, -1, -1):
        result = jnp.where(chunk == index, values[index], result)
    return result


def kernel(
    tokens, out_grad, routes, gates, w_gu, w_dn,
    moe_out, tokens_grad, wgu_out, wdn_out,
    tg, pick_all, gate_all, pick_c, gate_hi, gate_lo,
    x_send, x_recv, rows, wgu, wdn, part, rs_send, rs_recv, act, fin, r_recv, wgu_st, wdn_st,
    ld_sem, xs_sem, xr_sem, rss_sem, rsr_sem, ags_sem, agr_sem, rts_sem, rtr_sem, out_sem,
):
    ctx = lax.axis_index("ctx")
    tp = lax.axis_index("tp")
    n_ctx = SIDE * SIDE * CORES
    core = lax.rem(ctx, CORES)
    my_y = lax.rem(ctx // CORES, SIDE)
    my_x = ctx // (CORES * SIDE)
    up = lax.rem(tp + 1, RING)
    down = lax.rem(tp + RING - 1, RING)
    top, tok = routes.shape
    width = tokens.shape[1]
    ff = wdn.shape[1]
    cap = x_send.shape[2] // 2
    block = 2 * cap
    exp_rows = n_ctx * cap
    half_rows = SPOTS * cap
    strip = ff // 2
    wide = 3 * strip
    cuts = ((wide // 128 + 1) // 2 * 128, wide // 256 * 128)
    experts = 2 * n_ctx

    barrier = pltpu.get_barrier_semaphore()

    def greet(i, carry):
        pl.semaphore_signal(
            barrier, inc=1, device_id=(lax.rem(ctx + 1 + i, n_ctx), tp), device_id_type=MESH
        )
        return carry

    lax.fori_loop(0, n_ctx - 1, greet, 0)
    pl.semaphore_signal(barrier, inc=1, device_id=(ctx, up), device_id_type=MESH)
    pl.semaphore_signal(barrier, inc=1, device_id=(ctx, down), device_id_type=MESH)

    loads = [
        pltpu.make_async_copy(tokens, tg.at[:, pl.ds(0, width)], ld_sem.at[0]),
        pltpu.make_async_copy(out_grad, tg.at[:, pl.ds(width, width)], ld_sem.at[1]),
        pltpu.make_async_copy(w_dn, wdn, ld_sem.at[2]),
    ]
    for t in range(2):
        for u in range(2):
            loads.append(
                pltpu.make_async_copy(
                    w_gu.at[:, :, pl.ds(u * ff + t * strip, strip)],
                    wgu.at[:, :, pl.ds(t * ff + u * strip, strip)],
                    ld_sem.at[3 + 2 * t + u],
                )
            )
    for load in loads:
        load.start()

    ids = lax.broadcasted_iota(jnp.int32, (experts, tok), 0)
    named = jnp.zeros((experts, tok), F32)
    gate_t = jnp.zeros((experts, tok), F32)
    for k in range(top):
        hit = routes[k : k + 1, :] == ids
        named = named + jnp.where(hit, 1.0, 0.0)
        gate_t = gate_t + jnp.where(hit, gates[k : k + 1, :], 0.0)
    before = (
        lax.broadcasted_iota(jnp.int32, (tok, tok), 0)
        < lax.broadcasted_iota(jnp.int32, (tok, tok), 1)
    )
    earlier = dot(named.astype(BF), jnp.where(before, 1.0, 0.0).astype(BF))
    slot = jnp.where(named > 0.5, earlier, -1.0)
    group = 8
    for g in range(experts // group):
        part_slot = slot[g * group : (g + 1) * group][:, None, :]
        part_gate = gate_t[g * group : (g + 1) * group][:, None, :]
        wanted = lax.broadcasted_iota(jnp.int32, (group, cap, tok), 1).astype(F32)
        owned = part_slot == wanted
        span = pl.ds(g * group * cap, group * cap)
        pick_all[span, :] = jnp.where(owned, 1.0, 0.0).reshape(group * cap, tok).astype(BF)
        gate_all[span, :] = jnp.where(owned, part_gate, 0.0).reshape(group * cap, tok)
    loads[0].wait()
    loads[1].wait()

    def peer(chunk, q, sign):
        if isinstance(q, int):
            dx = pick(chunk, [OFFSETS[c][q][0] for c in range(CHUNKS)])
            dy = pick(chunk, [OFFSETS[c][q][1] for c in range(CHUNKS)])
        else:
            dx = pick(q, [offset[0] for offset in OFFSETS[chunk]])
            dy = pick(q, [offset[1] for offset in OFFSETS[chunk]])
        px = lax.rem(my_x + sign * dx + SIDE, SIDE)
        py = lax.rem(my_y + sign * dy + SIDE, SIDE)
        return (px * SIDE + py) * CORES

    def dispatch(chunk, i):
        q, b = i // 2, i % 2
        return pltpu.make_async_remote_copy(
            src_ref=x_send.at[chunk, i], dst_ref=x_recv.at[chunk, 2 * q + core],
            send_sem=xs_sem.at[chunk, i], recv_sem=xr_sem.at[chunk, 2 * q + core],
            device_id=(peer(chunk, q, -1) + b, tp), device_id_type=MESH,
        )

    def arrival(chunk, i):
        return pltpu.make_async_remote_copy(
            src_ref=x_send.at[chunk, i], dst_ref=x_recv.at[chunk, i],
            send_sem=xs_sem.at[chunk, i], recv_sem=xr_sem.at[chunk, i],
            device_id=(peer(chunk, i // 2, 1) + i % 2, tp), device_id_type=MESH,
        )

    def back(chunk, i, q=None):
        q, b = i // 2 if q is None else q, i % 2
        i = 2 * q + b
        return pltpu.make_async_remote_copy(
            src_ref=x_send.at[chunk, i], dst_ref=r_recv.at[chunk, 2 * q + core],
            send_sem=rts_sem.at[chunk, i], recv_sem=rtr_sem.at[chunk, 2 * q + core],
            device_id=(peer(chunk, q, 1) + b, tp), device_id_type=MESH,
        )

    def back_arrival(chunk, i):
        return pltpu.make_async_remote_copy(
            src_ref=x_send.at[chunk, i], dst_ref=r_recv.at[chunk, i],
            send_sem=rts_sem.at[chunk, i], recv_sem=rtr_sem.at[chunk, i],
            device_id=(peer(chunk, i // 2, -1) + i % 2, tp), device_id_type=MESH,
        )

    def remote_only(chunk, i, act_on):
        if i < 2:
            pl.when(jnp.logical_or(chunk != 0, core != i))(act_on)
        else:
            act_on()

    def build(chunk):
        for i in range(SPOTS):
            dest = peer(chunk, i // 2, -1) + i % 2
            span = pl.ds(pl.multiple_of(dest * block, block), block)
            here = pl.ds(i * block, block)
            pick_c[chunk, here, :] = pick_all[span, :]
            weights = gate_all[span, :]
            high = weights.astype(BF)
            gate_hi[chunk, here, :] = high
            gate_lo[chunk, here, :] = (weights - high.astype(F32)).astype(BF)
            fin[pl.ds(i * block, block), 0:1] = jnp.sum(weights, axis=1, keepdims=True)
        chosen = dot(pick_c[chunk], tg[:, 0:width])
        x_send[chunk, :, :, 0:width] = chosen.astype(BF).reshape(SPOTS, block, width)
        chosen = dot(pick_c[chunk], tg[:, width : 2 * width]) * fin[:, 0:1]
        x_send[chunk, :, :, width : 2 * width] = chosen.astype(BF).reshape(SPOTS, block, width)

    def send_rows(chunk):
        for i in range(SPOTS):
            remote_only(chunk, i, lambda i=i: dispatch(chunk, i).start())

    def take_rows(chunk):
        for i in range(SPOTS):
            remote_only(chunk, i, lambda i=i: arrival(chunk, i).wait_recv())
        for pair in range(SPOTS // 2):
            first = x_recv[chunk, 2 * pair].astype(F32)
            second = x_recv[chunk, 2 * pair + 1].astype(F32)
            for e in range(2):
                both = jnp.concatenate(
                    [first[e * cap : (e + 1) * cap], second[e * cap : (e + 1) * cap]], axis=0
                )
                start = e * exp_rows + chunk * half_rows + pair * block
                rows[pl.ds(pl.multiple_of(start, 16), block), :] = both.astype(BF)

    def products(chunk):
        side = lax.rem(chunk, 2)
        for e in range(2):
            span = pl.ds(pl.multiple_of(e * exp_rows + chunk * half_rows, 16), half_rows)
            out = pl.ds(e * half_rows, half_rows)
            left, grads = rows[span, 0:width], rows[span, width : 2 * width]
            for t in range(2):
                part[side, t, out, 0 : 2 * strip] = dot(left, wgu[e, :, t * ff : (t + 1) * ff])
                part[side, t, out, 2 * strip : wide] = dot(
                    grads, wdn[e, t * strip : (t + 1) * strip, :], 1, 1
                )

    def own_rows(owner):
        return pl.ds(pl.multiple_of(owner * block, block), block)

    def cut(t, way):
        return pl.ds(0, cuts[t]) if way == 0 else pl.ds(cuts[t], wide - cuts[t])

    def rs_copy(chunk, t, way, step):
        side = lax.rem(chunk, 2)
        src, dst = rs_send.at[side, t, way, step], rs_recv.at[chunk, t, way, step]
        if step == 0:
            src, dst = src.at[:, cut(t, way)], dst.at[:, cut(t, way)]
        return pltpu.make_async_remote_copy(
            src_ref=src, dst_ref=dst,
            send_sem=rss_sem.at[chunk, t, way, step], recv_sem=rsr_sem.at[chunk, t, way, step],
            device_id=(ctx, (up, down)[way]), device_id_type=MESH,
        )

    def rs_drain(chunk, t):
        for way in range(2):
            for step in range(4):
                rs_copy(chunk, t, way, step).wait_send()

    def rs_step(chunk, t, step):
        side = lax.rem(chunk, 2)
        if step == 0:
            pl.when(chunk >= 2)(lambda: rs_drain(chunk - 2, t))
        for way in range(2):
            owner = lax.rem(tp + (4 - step if way == 0 else 4 + step), RING)
            mine = own_rows(owner)
            if step == 0:
                cols = cut(t, way)
                rs_send[side, t, way, 0, :, cols] = part[side, t, mine, cols].astype(BF)
            else:
                rs_copy(chunk, t, way, step - 1).wait_recv()
                for w in range(2):
                    cols = cut(t, w)
                    value = part[side, t, mine, cols]
                    if step > 1 or w == way:
                        value = value + rs_recv[chunk, t, way, step - 1, :, cols].astype(F32)
                    rs_send[side, t, way, step, :, cols] = value.astype(BF)
            rs_copy(chunk, t, way, step).start()

    def act_rows(chunk, owner):
        start = (owner // 4) * exp_rows + chunk * half_rows + lax.rem(owner, 4) * block
        return pl.ds(pl.multiple_of(start, 16), block)

    def rs_last(chunk, t):
        side = lax.rem(chunk, 2)
        for way in range(2):
            rs_copy(chunk, t, way, 3).wait_recv()

        def total(s):
            cols = slice(s * strip, (s + 1) * strip)
            value = part[side, t, own_rows(tp), cols]
            for way in range(2):
                value = value + rs_recv[chunk, t, way, 3, :, cols].astype(F32)
            return value

        out = act_rows(chunk, tp)
        gate, upper, grad = total(0), total(1), total(2)
        sigma = jax.nn.sigmoid(gate)
        silu = gate * sigma
        act[t, out, 0:strip] = (silu * upper).astype(BF)
        act[t, out, strip : 2 * strip] = (
            grad * upper * sigma * (1.0 + gate * (1.0 - sigma))
        ).astype(BF)
        act[t, out, 2 * strip : wide] = (grad * silu).astype(BF)

    def ag_move(chunk, t, way, step, owner):
        ref = act.at[t, act_rows(chunk, lax.rem(owner, RING))]
        if step == 3:
            ref = ref.at[:, cut(t, way)]
        return pltpu.make_async_remote_copy(
            src_ref=ref, dst_ref=ref,
            send_sem=ags_sem.at[chunk, t, way, step], recv_sem=agr_sem.at[chunk, t, way, step],
            device_id=(ctx, (up, down)[way]), device_id_type=MESH,
        )

    def ag_copy(chunk, t, way, step):
        return ag_move(chunk, t, way, step, tp + (RING - step if way == 0 else step))

    def ag_arrival(chunk, t, way, step):
        return ag_move(chunk, t, way, step, tp + (RING - step - 1 if way == 0 else step + 1))

    def ag_step(chunk, t, step):
        if step == 0:
            rs_last(chunk, t)
        for way in range(2):
            if step > 0:
                ag_arrival(chunk, t, way, step - 1).wait_recv()
            ag_copy(chunk, t, way, step).start()

    def ag_last(chunk, t):
        for way in range(2):
            ag_arrival(chunk, t, way, 3).wait_recv()

    def rows_out(e, span):
        outs = dot(act[0, span, 0:strip], wdn[e, 0:strip, :]) + dot(
            act[1, span, 0:strip], wdn[e, strip : 2 * strip, :]
        )
        grads = dot(act[0, span, strip:wide], wgu[e, :, 0:ff], 1, 1) + dot(
            act[1, span, strip:wide], wgu[e, :, ff : 2 * ff], 1, 1
        )
        return outs, grads

    def finish_pair(q):
        chunk = CHUNKS - 1
        for e in range(2):
            start = e * exp_rows + chunk * half_rows + q * block
            out = pl.ds(e * block, block)
            outs, grads = rows_out(e, pl.ds(pl.multiple_of(start, 16), block))
            fin[out, 0:width] = outs
            fin[out, width : 2 * width] = grads
        for b in range(2):
            at = b * cap
            both = jnp.concatenate([fin[at : at + cap, :], fin[block + at : block + at + cap, :]], axis=0)
            x_send[chunk, 2 * q + b] = both.astype(BF)
            back(chunk, b, q).start()

    def finish(chunk):
        ag_last(chunk, 0)
        ag_last(chunk, 1)
        for i in range(SPOTS):
            remote_only(chunk, i, lambda i=i: dispatch(chunk, i).wait_send())
        for e in range(2):
            span = pl.ds(pl.multiple_of(e * exp_rows + chunk * half_rows, 16), half_rows)
            out = pl.ds(e * half_rows, half_rows)
            outs, grads = rows_out(e, span)
            fin[out, 0:width] = outs
            fin[out, width : 2 * width] = grads
        for i in range(SPOTS):
            both = jnp.concatenate(
                [
                    fin[i * cap : (i + 1) * cap, :],
                    fin[half_rows + i * cap : half_rows + (i + 1) * cap, :],
                ],
                axis=0,
            )
            x_send[chunk, i] = both.astype(BF)
            remote_only(chunk, i, lambda i=i: back(chunk, i).start())

    build(0)
    pl.semaphore_wait(barrier, n_ctx + 1)
    send_rows(0)
    x_recv[0, core] = x_send[0, core]
    build(1)
    for load in loads[2:]:
        load.wait()
    take_rows(0)
    send_rows(1)
    products(0)

    def turn(c, carry):
        for t in range(2):
            before_c = c - 1 if t == 0 else c
            for a in range(2):

                @pl.when(jnp.logical_and(before_c >= 1, before_c <= CHUNKS))
                def _():
                    ag_step(before_c - 1, 1 - t, 2 + a)

                @pl.when(jnp.logical_and(c >= 1, c <= CHUNKS))
                def _():
                    ag_step(c - 1, t, a)

                @pl.when(jnp.logical_and(before_c >= 0, before_c < CHUNKS))
                def _():
                    rs_step(before_c, 1 - t, 2 + a)

                @pl.when(c < CHUNKS)
                def _():
                    rs_step(c, t, a)

                if (t, a) == (1, 0):

                    @pl.when(c + 2 < CHUNKS)
                    def _():
                        build(c + 2)
                        send_rows(c + 2)

                    pl.when(c >= 2)(lambda: finish(c - 2))

                if (t, a) == (1, 1):

                    @pl.when(c + 1 < CHUNKS)
                    def _():
                        take_rows(c + 1)
                        products(c + 1)

        return carry

    lax.fori_loop(0, CHUNKS + 1, turn, 0)

    stores = []

    def store(src, dst):
        stores.append(pltpu.make_async_copy(src, dst, out_sem.at[len(stores)]))
        stores[-1].start()

    def weight_grads(t):
        for e in range(2):
            span = slice(e * exp_rows, (e + 1) * exp_rows)
            wgu_st[e, :, t * ff : (t + 1) * ff] = dot(
                rows[span, 0:width], act[t, span, strip:wide], 0, 0
            ).astype(BF)
            for u in range(2):
                store(
                    wgu_st.at[e, :, pl.ds(t * ff + u * strip, strip)],
                    wgu_out.at[e, :, pl.ds(u * ff + t * strip, strip)],
                )
            wdn_st[e, t * strip : (t + 1) * strip, :] = dot(
                act[t, span, 0:strip], rows[span, width : 2 * width], 0, 0
            ).astype(BF)
            at = pl.ds(t * strip, strip)
            store(wdn_st.at[e, at], wdn_out.at[e, at])

    def combine(chunk):
        for i in range(SPOTS):
            remote_only(chunk, i, lambda: back_arrival(chunk, i).wait_recv())
        came = r_recv[chunk, :, :, 0:width].reshape(SPOTS * block, width)
        outs = dot(gate_hi[chunk], came, 0, 0) + dot(gate_lo[chunk], came, 0, 0)
        came = r_recv[chunk, :, :, width : 2 * width].reshape(SPOTS * block, width)
        grads = dot(pick_c[chunk], came, 0, 0)
        if chunk > 0:
            outs, grads = fin[0:tok, 0:width] + outs, fin[0:tok, width : 2 * width] + grads
        return outs, grads

    last = CHUNKS - 1
    for i in range(SPOTS):
        dispatch(last, i).wait_send()
    ag_step(last, 1, 2)
    ag_last(last, 0)
    finish_pair(lax.rem(tp + 2, 4))
    ag_step(last, 1, 3)
    finish_pair(lax.rem(tp + 1, 4))
    finish_pair(lax.rem(tp + 3, 4))
    weight_grads(0)
    ag_last(last, 1)
    finish_pair(lax.rem(tp, 4))
    weight_grads(1)

    r_recv[0, core] = x_send[0, core]
    for chunk in range(CHUNKS):
        outs, grads = combine(chunk)
        if chunk < last:
            fin[0:tok, 0:width] = outs
            fin[0:tok, width : 2 * width] = grads
    moe_out[...] = outs.astype(BF)
    tokens_grad[...] = grads.astype(BF)

    for chunk in range(CHUNKS):
        for t in range(2):
            for way in range(2):
                for step in range(4):
                    ag_copy(chunk, t, way, step).wait_send()
        for i in range(SPOTS):
            remote_only(chunk, i, lambda i=i, chunk=chunk: back(chunk, i).wait_send())
    for chunk in range(CHUNKS - 2, CHUNKS):
        for t in range(2):
            rs_drain(chunk, t)
    for copy in stores:
        copy.wait()


def hand_on(*refs):
    count = (len(refs) - 2) // 3
    came, left = refs[-2:]
    loads, stores = [], []
    for src, dst, mid in zip(refs[:count], refs[count : 2 * count], refs[2 * count : 3 * count]):
        pieces = 8 if len(src.shape) == 3 else 1
        for piece in range(pieces):
            views = [src, mid, dst]
            if pieces > 1:
                depth = src.shape[1] // 4
                at = pl.ds(piece % 4 * depth, depth)
                views = [view.at[piece // 4, at] for view in views]
            loads.append(pltpu.make_async_copy(views[0], views[1], came.at[len(loads)]))
            stores.append(pltpu.make_async_copy(views[1], views[2], left.at[len(stores)]))
            loads[-1].start()
    for load, copy in zip(loads, stores):
        load.wait()
        copy.start()
    for copy in stores:
        copy.wait()


def body(tokens, out_grad, routes, gates, w_gu, w_dn):
    tok, width = tokens.shape
    top = routes.shape[1]
    routes, gates = routes.T, gates.T
    ff = w_dn.shape[1]
    n_ctx = SIDE * SIDE * CORES
    cap = 3 * tok * top // (4 * n_ctx)
    block = 2 * cap
    chunk_rows = SPOTS * block
    all_rows = CHUNKS * chunk_rows
    wide = 3 * ff // 2
    dma = pltpu.SemaphoreType.DMA
    any_space = pl.BlockSpec(memory_space=pl.ANY)
    vmem = pl.BlockSpec(memory_space=pltpu.VMEM)
    flops = 6 * all_rows * width * 3 * ff
    results = pl.pallas_call(
        kernel,
        out_shape=(
            jax.ShapeDtypeStruct((tok, width), BF),
            jax.ShapeDtypeStruct((tok, width), BF),
            jax.ShapeDtypeStruct(w_gu.shape, BF),
            jax.ShapeDtypeStruct(w_dn.shape, BF),
        ),
        in_specs=[any_space, any_space, vmem, vmem, any_space, any_space],
        out_specs=(vmem, vmem, any_space, any_space),
        scratch_shapes=[
            pltpu.VMEM((tok, 2 * width), BF),
            pltpu.VMEM((all_rows, tok), BF),
            pltpu.VMEM((all_rows, tok), F32),
            pltpu.VMEM((CHUNKS, chunk_rows, tok), BF),
            pltpu.VMEM((CHUNKS, chunk_rows, tok), BF),
            pltpu.VMEM((CHUNKS, chunk_rows, tok), BF),
            pltpu.VMEM((CHUNKS, SPOTS, block, 2 * width), BF),
            pltpu.VMEM((CHUNKS, SPOTS, block, 2 * width), BF),
            pltpu.VMEM((all_rows, 2 * width), BF),
            pltpu.VMEM(w_gu.shape, BF),
            pltpu.VMEM(w_dn.shape, BF),
            pltpu.VMEM((2, 2, chunk_rows, wide), F32),
            pltpu.VMEM((2, 2, 2, 4, block, wide), BF),
            pltpu.VMEM((CHUNKS, 2, 2, 4, block, wide), BF),
            pltpu.VMEM((2, all_rows, wide), BF),
            pltpu.VMEM((chunk_rows, 2 * width), F32),
            pltpu.VMEM((CHUNKS, SPOTS, block, 2 * width), BF),
            pltpu.VMEM(w_gu.shape, BF),
            pltpu.VMEM(w_dn.shape, BF),
            dma((7,)),
            dma((CHUNKS, SPOTS)),
            dma((CHUNKS, SPOTS)),
            dma((CHUNKS, 2, 2, 4)),
            dma((CHUNKS, 2, 2, 4)),
            dma((CHUNKS, 2, 2, 4)),
            dma((CHUNKS, 2, 2, 4)),
            dma((CHUNKS, SPOTS)),
            dma((CHUNKS, SPOTS)),
            dma((12,)),
        ],
        compiler_params=pltpu.CompilerParams(
            collective_id=0, has_side_effects=True, vmem_limit_bytes=60 * 1024 * 1024
        ),
        cost_estimate=pl.CostEstimate(flops=flops, bytes_accessed=10 << 20, transcendentals=0),
        name="moe",
    )(tokens, out_grad, routes, gates, w_gu, w_dn)
    return pl.pallas_call(
        hand_on,
        out_shape=tuple(jax.ShapeDtypeStruct(r.shape, r.dtype) for r in results),
        in_specs=[any_space] * 4,
        out_specs=(any_space,) * 4,
        scratch_shapes=[pltpu.VMEM(r.shape, r.dtype) for r in results] + [dma((18,)), dma((18,))],
        compiler_params=pltpu.CompilerParams(vmem_limit_bytes=60 * 1024 * 1024),
        name="hand_on",
    )(*results)


def solution(mesh):
    return jax.shard_map(
        body,
        mesh=mesh,
        in_specs=(
            P("ctx", "tp"),
            P("ctx", "tp"),
            P("ctx", None),
            P("ctx", None),
            P("ctx", "tp", None),
            P("ctx", None, "tp"),
        ),
        out_specs=(P("ctx", "tp"), P("ctx", "tp"), P("ctx", "tp", None), P("ctx", None, "tp")),
        check_vma=False,
    )
```

time: 213 us -> 186 us (0.87)
  Pallas kernels: 201 us -> 185 us
  local copies, waits for them, and re-layouts: 11 us -> 0 us
    pallas_call x1, Pallas kernels: 201 us -> 180 us  [body(): pl.pallas_call(kernel, out_shape=(jax.ShapeDtypeStruct((tok, width), BF),...]
    unnamed x8 -> x0, local copies, waits for them, and re-layouts: 11 us -> none
    pallas_call x0 -> x1, Pallas kernels: none -> 4.72 us  [body(): pl.pallas_call(hand_on, out_shape=tuple((jax.ShapeDtypeStruct(r.shape, r....]
where the time goes in v2:
time: 186 us
  Pallas kernels  185 us (99%)
    pallas_call x1, Pallas kernels, body(): pl.pallas_call(kernel, out_shape=(jax.ShapeDtypeStruct((tok, width), BF),...  180 us
    pallas_call x1, Pallas kernels, body(): pl.pallas_call(hand_on, out_shape=tuple((jax.ShapeDtypeStruct(r.shape, r....  4.72 us

profile of v2, /device:TPU:1, one launch (start us, length us, event | category | flops | bytes accessed | tf_op | source)
XLA Modules:
  0.0 185.7 jit_solution(13726393601623974577)
XLA Ops:
  0.6 180.2 %moe.1 = (bf16[128,512]{1,0:T(8,128)(2,1)}, bf16[128,512]{1,0:T(8,128)(2,1)}, bf16[2,512,1536]{2,1,0:T(8,128)(2,1)}, bf16[2,768,512]{2,1,0:T(8,128)(2,1)}) custom-call(bf16[128,512]{1,0:T(8,128)(2,1)} %tokens.1, bf16[128,512]{1,0:T(8,128)(2,1)} %out_grad.1, s32[8,128]{1,0:T(8,128)} %bitcast.2, f32[8,128]{1,0:T(8,128)} %bitcast.3, ...), custom_call_target="tpu_custom_call" | custom-call | flops 10871635968 | bytes 10485760 | tf_op jit(solution)/shard_map/moe/pallas_call | solution.py:513
  180.8 4.7 %hand_on.1 = (bf16[128,512]{1,0:T(8,128)(2,1)}, bf16[128,512]{1,0:T(8,128)(2,1)}, bf16[2,512,1536]{2,1,0:T(8,128)(2,1)}, bf16[2,768,512]{2,1,0:T(8,128)(2,1)}) custom-call(bf16[128,512]{1,0:T(8,128)(2,1)} %get-tuple-element.8.refs_0_, bf16[128,512]{1,0:T(8,128)(2,1)} %get-tuple-element.9.refs_1_, bf16[2,512,1536]{2,1,0:T(8,128)(2,1)} %get-tuple-element.10.refs_2_, ...), custom_call_target="tpu_custom_call" | custom-call | tf_op jit(solution)/shard_map/hand_on/pallas_call | solution.py:560

commit v3 on v2

--- a/solution.py
+++ b/solution.py
@@ -36,9 +36,9 @@
 
 
 def kernel(
-    tokens, out_grad, routes, gates, w_gu, w_dn,
+    tokens, out_grad, routes_in, gates_in, w_gu, w_dn,
     moe_out, tokens_grad, wgu_out, wdn_out,
-    tg, pick_all, gate_all, pick_c, gate_hi, gate_lo,
+    routes, gates, tg, pick_all, gate_all, pick_c, gate_hi, gate_lo,
     x_send, x_recv, rows, wgu, wdn, part, rs_send, rs_recv, act, fin, r_recv, wgu_st, wdn_st,
     ld_sem, xs_sem, xr_sem, rss_sem, rsr_sem, ags_sem, agr_sem, rts_sem, rtr_sem, out_sem,
 ):
@@ -50,7 +50,7 @@
     my_x = ctx // (CORES * SIDE)
     up = lax.rem(tp + 1, RING)
     down = lax.rem(tp + RING - 1, RING)
-    top, tok = routes.shape
+    top, tok = routes_in.shape
     width = tokens.shape[1]
     ff = wdn.shape[1]
     cap = x_send.shape[2] // 2
@@ -59,7 +59,7 @@
     half_rows = SPOTS * cap
     strip = ff // 2
     wide = 3 * strip
-    cuts = ((wide // 128 + 1) // 2 * 128, wide // 256 * 128)
+    cuts = (2 * block // 3, block // 3)
     experts = 2 * n_ctx
 
     barrier = pltpu.get_barrier_semaphore()
@@ -88,8 +88,14 @@
                     ld_sem.at[3 + 2 * t + u],
                 )
             )
-    for load in loads:
+    tables = [
+        pltpu.make_async_copy(routes_in, routes, ld_sem.at[7]),
+        pltpu.make_async_copy(gates_in, gates, ld_sem.at[8]),
+    ]
+    for load in tables + loads:
         load.start()
+    for load in tables:
+        load.wait()
 
     ids = lax.broadcasted_iota(jnp.int32, (experts, tok), 0)
     named = jnp.zeros((experts, tok), F32)
@@ -197,29 +203,32 @@
                 start = e * exp_rows + chunk * half_rows + pair * block
                 rows[pl.ds(pl.multiple_of(start, 16), block), :] = both.astype(BF)
 
-    def products(chunk):
+    def products(chunk, t):
         side = lax.rem(chunk, 2)
         for e in range(2):
             span = pl.ds(pl.multiple_of(e * exp_rows + chunk * half_rows, 16), half_rows)
             out = pl.ds(e * half_rows, half_rows)
             left, grads = rows[span, 0:width], rows[span, width : 2 * width]
-            for t in range(2):
-                part[side, t, out, 0 : 2 * strip] = dot(left, wgu[e, :, t * ff : (t + 1) * ff])
-                part[side, t, out, 2 * strip : wide] = dot(
-                    grads, wdn[e, t * strip : (t + 1) * strip, :], 1, 1
-                )
+            part[side, t, out, 0 : 2 * strip] = dot(left, wgu[e, :, t * ff : (t + 1) * ff])
+            part[side, t, out, 2 * strip : wide] = dot(
+                grads, wdn[e, t * strip : (t + 1) * strip, :], 1, 1
+            )
 
     def own_rows(owner):
         return pl.ds(pl.multiple_of(owner * block, block), block)
 
     def cut(t, way):
-        return pl.ds(0, cuts[t]) if way == 0 else pl.ds(cuts[t], wide - cuts[t])
+        return (0, cuts[t]) if way == 0 else (cuts[t], block - cuts[t])
+
+    def some(start, t, way):
+        first, count = cut(t, way)
+        return pl.ds(pl.multiple_of(start + first, 16), count)
 
     def rs_copy(chunk, t, way, step):
         side = lax.rem(chunk, 2)
         src, dst = rs_send.at[side, t, way, step], rs_recv.at[chunk, t, way, step]
         if step == 0:
-            src, dst = src.at[:, cut(t, way)], dst.at[:, cut(t, way)]
+            src, dst = src.at[pl.ds(*cut(t, way))], dst.at[pl.ds(*cut(t, way))]
         return pltpu.make_async_remote_copy(
             src_ref=src, dst_ref=dst,
             send_sem=rss_sem.at[chunk, t, way, step], recv_sem=rsr_sem.at[chunk, t, way, step],
@@ -237,23 +246,23 @@
             pl.when(chunk >= 2)(lambda: rs_drain(chunk - 2, t))
         for way in range(2):
             owner = lax.rem(tp + (4 - step if way == 0 else 4 + step), RING)
-            mine = own_rows(owner)
-            if step == 0:
-                cols = cut(t, way)
-                rs_send[side, t, way, 0, :, cols] = part[side, t, mine, cols].astype(BF)
-            else:
+            if step > 0:
                 rs_copy(chunk, t, way, step - 1).wait_recv()
-                for w in range(2):
-                    cols = cut(t, w)
-                    value = part[side, t, mine, cols]
-                    if step > 1 or w == way:
-                        value = value + rs_recv[chunk, t, way, step - 1, :, cols].astype(F32)
-                    rs_send[side, t, way, step, :, cols] = value.astype(BF)
+            for w in range(2):
+                if step == 0 and w != way:
+                    continue
+                value = part[side, t, some(owner * block, t, w), :]
+                here = pl.ds(*cut(t, w))
+                if step > 1 or (step == 1 and w == way):
+                    value = value + rs_recv[chunk, t, way, step - 1, here, :].astype(F32)
+                rs_send[side, t, way, step, here, :] = value.astype(BF)
             rs_copy(chunk, t, way, step).start()
 
+    def act_start(chunk, owner):
+        return (owner // 4) * exp_rows + chunk * half_rows + lax.rem(owner, 4) * block
+
     def act_rows(chunk, owner):
-        start = (owner // 4) * exp_rows + chunk * half_rows + lax.rem(owner, 4) * block
-        return pl.ds(pl.multiple_of(start, 16), block)
+        return pl.ds(pl.multiple_of(act_start(chunk, owner), 16), block)
 
     def rs_last(chunk, t):
         side = lax.rem(chunk, 2)
@@ -278,9 +287,8 @@
         act[t, out, 2 * strip : wide] = (grad * silu).astype(BF)
 
     def ag_move(chunk, t, way, step, owner):
-        ref = act.at[t, act_rows(chunk, lax.rem(owner, RING))]
-        if step == 3:
-            ref = ref.at[:, cut(t, way)]
+        start = act_start(chunk, lax.rem(owner, RING))
+        ref = act.at[t, pl.ds(pl.multiple_of(start, 16), block) if step < 3 else some(start, t, way)]
         return pltpu.make_async_remote_copy(
             src_ref=ref, dst_ref=ref,
             send_sem=ags_sem.at[chunk, t, way, step], recv_sem=agr_sem.at[chunk, t, way, step],
@@ -359,48 +367,39 @@
         load.wait()
     take_rows(0)
     send_rows(1)
-    products(0)
+    products(0, 0)
 
     def turn(c, carry):
-        for t in range(2):
-            before_c = c - 1 if t == 0 else c
-            for a in range(2):
-
-                @pl.when(jnp.logical_and(before_c >= 1, before_c <= CHUNKS))
+        for step in range(4):
+
+            @pl.when(c >= 1)
+            def _():
+                ag_step(c - 1, 0, step)
+                ag_step(c - 1, 1, step)
+
+            rs_step(c, 0, step)
+            if step == 0:
+                products(c, 1)
+            rs_step(c, 1, step)
+            if step == 0:
+                pl.when(c >= 2)(lambda: finish(c - 2))
+            if step == 1:
+
+                @pl.when(c + 2 < CHUNKS)
                 def _():
-                    ag_step(before_c - 1, 1 - t, 2 + a)
-
-                @pl.when(jnp.logical_and(c >= 1, c <= CHUNKS))
+                    build(c + 2)
+                    send_rows(c + 2)
+
+            if step == 3:
+
+                @pl.when(c + 1 < CHUNKS)
                 def _():
-                    ag_step(c - 1, t, a)
-
-                @pl.when(jnp.logical_and(before_c >= 0, before_c < CHUNKS))
-                def _():
-                    rs_step(before_c, 1 - t, 2 + a)
-
-                @pl.when(c < CHUNKS)
-                def _():
-                    rs_step(c, t, a)
-
-                if (t, a) == (1, 0):
-
-                    @pl.when(c + 2 < CHUNKS)
-                    def _():
-                        build(c + 2)
-                        send_rows(c + 2)
-
-                    pl.when(c >= 2)(lambda: finish(c - 2))
-
-                if (t, a) == (1, 1):
-
-                    @pl.when(c + 1 < CHUNKS)
-                    def _():
-                        take_rows(c + 1)
-                        products(c + 1)
+                    take_rows(c + 1)
+                    products(c + 1, 0)
 
         return carry
 
-    lax.fori_loop(0, CHUNKS + 1, turn, 0)
+    lax.fori_loop(0, CHUNKS, turn, 0)
 
     stores = []
 
@@ -408,22 +407,21 @@
         stores.append(pltpu.make_async_copy(src, dst, out_sem.at[len(stores)]))
         stores[-1].start()
 
-    def weight_grads(t):
-        for e in range(2):
-            span = slice(e * exp_rows, (e + 1) * exp_rows)
-            wgu_st[e, :, t * ff : (t + 1) * ff] = dot(
-                rows[span, 0:width], act[t, span, strip:wide], 0, 0
-            ).astype(BF)
-            for u in range(2):
-                store(
-                    wgu_st.at[e, :, pl.ds(t * ff + u * strip, strip)],
-                    wgu_out.at[e, :, pl.ds(u * ff + t * strip, strip)],
-                )
-            wdn_st[e, t * strip : (t + 1) * strip, :] = dot(
-                act[t, span, 0:strip], rows[span, width : 2 * width], 0, 0
-            ).astype(BF)
-            at = pl.ds(t * strip, strip)
-            store(wdn_st.at[e, at], wdn_out.at[e, at])
+    def weight_grads(t, e):
+        span = slice(e * exp_rows, (e + 1) * exp_rows)
+        wgu_st[e, :, t * ff : (t + 1) * ff] = dot(
+            rows[span, 0:width], act[t, span, strip:wide], 0, 0
+        ).astype(BF)
+        for u in range(2):
+            store(
+                wgu_st.at[e, :, pl.ds(t * ff + u * strip, strip)],
+                wgu_out.at[e, :, pl.ds(u * ff + t * strip, strip)],
+            )
+        wdn_st[e, t * strip : (t + 1) * strip, :] = dot(
+            act[t, span, 0:strip], rows[span, width : 2 * width], 0, 0
+        ).astype(BF)
+        at = pl.ds(t * strip, strip)
+        store(wdn_st.at[e, at], wdn_out.at[e, at])
 
     def combine(chunk):
         for i in range(SPOTS):
@@ -439,16 +437,21 @@
     last = CHUNKS - 1
     for i in range(SPOTS):
         dispatch(last, i).wait_send()
-    ag_step(last, 1, 2)
-    ag_last(last, 0)
-    finish_pair(lax.rem(tp + 2, 4))
-    ag_step(last, 1, 3)
+    for step in range(4):
+        ag_step(last, 0, step)
+        ag_step(last, 1, step)
+        if step == 0:
+            finish(last - 1)
+        if step == 2:
+            finish_pair(lax.rem(tp + 2, 4))
     finish_pair(lax.rem(tp + 1, 4))
     finish_pair(lax.rem(tp + 3, 4))
-    weight_grads(0)
+    ag_last(last, 0)
     ag_last(last, 1)
     finish_pair(lax.rem(tp, 4))
-    weight_grads(1)
+    for t in range(2):
+        for e in range(2):
+            weight_grads(t, e)
 
     r_recv[0, core] = x_send[0, core]
     for chunk in range(CHUNKS):
@@ -478,13 +481,11 @@
     came, left = refs[-2:]
     loads, stores = [], []
     for src, dst, mid in zip(refs[:count], refs[count : 2 * count], refs[2 * count : 3 * count]):
-        pieces = 8 if len(src.shape) == 3 else 1
+        pieces = src.shape[0] if len(src.shape) == 3 else 1
         for piece in range(pieces):
             views = [src, mid, dst]
             if pieces > 1:
-                depth = src.shape[1] // 4
-                at = pl.ds(piece % 4 * depth, depth)
-                views = [view.at[piece // 4, at] for view in views]
+                views = [view.at[piece] for view in views]
             loads.append(pltpu.make_async_copy(views[0], views[1], came.at[len(loads)]))
             stores.append(pltpu.make_async_copy(views[1], views[2], left.at[len(stores)]))
             loads[-1].start()
@@ -518,9 +519,11 @@
             jax.ShapeDtypeStruct(w_gu.shape, BF),
             jax.ShapeDtypeStruct(w_dn.shape, BF),
         ),
-        in_specs=[any_space, any_space, vmem, vmem, any_space, any_space],
+        in_specs=[any_space] * 6,
         out_specs=(vmem, vmem, any_space, any_space),
         scratch_shapes=[
+            pltpu.VMEM(routes.shape, routes.dtype),
+            pltpu.VMEM(gates.shape, gates.dtype),
             pltpu.VMEM((tok, 2 * width), BF),
             pltpu.VMEM((all_rows, tok), BF),
             pltpu.VMEM((all_rows, tok), F32),
@@ -540,7 +543,7 @@
             pltpu.VMEM((CHUNKS, SPOTS, block, 2 * width), BF),
             pltpu.VMEM(w_gu.shape, BF),
             pltpu.VMEM(w_dn.shape, BF),
-            dma((7,)),
+            dma((9,)),
             dma((CHUNKS, SPOTS)),
             dma((CHUNKS, SPOTS)),
             dma((CHUNKS, 2, 2, 4)),
@@ -562,7 +565,7 @@
         out_shape=tuple(jax.ShapeDtypeStruct(r.shape, r.dtype) for r in results),
         in_specs=[any_space] * 4,
         out_specs=(any_space,) * 4,
-        scratch_shapes=[pltpu.VMEM(r.shape, r.dtype) for r in results] + [dma((18,)), dma((18,))],
+        scratch_shapes=[pltpu.VMEM(r.shape, r.dtype) for r in results] + [dma((6,)), dma((6,))],
         compiler_params=pltpu.CompilerParams(vmem_limit_bytes=60 * 1024 * 1024),
         name="hand_on",
     )(*results)

time: 186 us -> 177 us (0.952)
  Pallas kernels: 185 us -> 175 us
    pallas_call x1, Pallas kernels: 180 us -> 171 us  [body(): pl.pallas_call(kernel, out_shape=(jax.ShapeDtypeStruct((tok, width), BF),...]
where the time goes in v3:
time: 177 us; the launch traced here: 176 us
  Pallas kernels  175 us (99%)
    pallas_call x1, Pallas kernels, body(): pl.pallas_call(kernel, out_shape=(jax.ShapeDtypeStruct((tok, width), BF),...  171 us
    pallas_call x1, Pallas kernels, body(): pl.pallas_call(hand_on, out_shape=tuple((jax.ShapeDtypeStruct(r.shape, r....  3.89 us

profile of v3, /device:TPU:1, one launch (start us, length us, event | category | flops | bytes accessed | tf_op | source)
XLA Modules:
  0.0 175.9 jit_solution(9164245428849908681)
XLA Ops:
  0.6 171.2 %moe.1 = (bf16[128,512]{1,0:T(8,128)(2,1)}, bf16[128,512]{1,0:T(8,128)(2,1)}, bf16[2,512,1536]{2,1,0:T(8,128)(2,1)}, bf16[2,768,512]{2,1,0:T(8,128)(2,1)}) custom-call(bf16[128,512]{1,0:T(8,128)(2,1)} %tokens.1, bf16[128,512]{1,0:T(8,128)(2,1)} %out_grad.1, s32[8,128]{1,0:T(8,128)} %bitcast.2, f32[8,128]{1,0:T(8,128)} %bitcast.3, ...), custom_call_target="tpu_custom_call" | custom-call | flops 10871635968 | bytes 10485760 | tf_op jit(solution)/shard_map/moe/pallas_call | solution.py:514
  171.8 3.9 %hand_on.1 = (bf16[128,512]{1,0:T(8,128)(2,1)}, bf16[128,512]{1,0:T(8,128)(2,1)}, bf16[2,512,1536]{2,1,0:T(8,128)(2,1)}, bf16[2,768,512]{2,1,0:T(8,128)(2,1)}) custom-call(bf16[128,512]{1,0:T(8,128)(2,1)} %get-tuple-element.8.refs_0_, bf16[128,512]{1,0:T(8,128)(2,1)} %get-tuple-element.9.refs_1_, bf16[2,512,1536]{2,1,0:T(8,128)(2,1)} %get-tuple-element.10.refs_2_, ...), custom_call_target="tpu_custom_call" | custom-call | tf_op jit(solution)/shard_map/hand_on/pallas_call | solution.py:563

commit v4 on v3

--- a/solution.py
+++ b/solution.py
@@ -39,7 +39,7 @@
     tokens, out_grad, routes_in, gates_in, w_gu, w_dn,
     moe_out, tokens_grad, wgu_out, wdn_out,
     routes, gates, tg, pick_all, gate_all, pick_c, gate_hi, gate_lo,
-    x_send, x_recv, rows, wgu, wdn, part, rs_send, rs_recv, act, fin, r_recv, wgu_st, wdn_st,
+    x_send, x_recv, rows, wgu, wdn, part, rs_send, rs_recv, act, fin, acc, r_recv, wgu_st, wdn_st,
     ld_sem, xs_sem, xr_sem, rss_sem, rsr_sem, ags_sem, agr_sem, rts_sem, rtr_sem, out_sem,
 ):
     ctx = lax.axis_index("ctx")
@@ -133,11 +133,19 @@
         py = lax.rem(my_y + sign * dy + SIDE, SIDE)
         return (px * SIDE + py) * CORES
 
+    def spot(q):
+        return 2 * ((q - core + 4) % 4) + core
+
+    def origin(chunk, k, b):
+        if isinstance(k, int):
+            return peer(chunk, (k + b) % 4, 1) + b
+        return peer(chunk, lax.rem(k + b, 4), 1) + b
+
     def dispatch(chunk, i):
         q, b = i // 2, i % 2
         return pltpu.make_async_remote_copy(
-            src_ref=x_send.at[chunk, i], dst_ref=x_recv.at[chunk, 2 * q + core],
-            send_sem=xs_sem.at[chunk, i], recv_sem=xr_sem.at[chunk, 2 * q + core],
+            src_ref=x_send.at[chunk, i], dst_ref=x_recv.at[chunk, spot(q)],
+            send_sem=xs_sem.at[chunk, i], recv_sem=xr_sem.at[chunk, spot(q)],
             device_id=(peer(chunk, q, -1) + b, tp), device_id_type=MESH,
         )
 
@@ -145,16 +153,15 @@
         return pltpu.make_async_remote_copy(
             src_ref=x_send.at[chunk, i], dst_ref=x_recv.at[chunk, i],
             send_sem=xs_sem.at[chunk, i], recv_sem=xr_sem.at[chunk, i],
-            device_id=(peer(chunk, i // 2, 1) + i % 2, tp), device_id_type=MESH,
-        )
-
-    def back(chunk, i, q=None):
-        q, b = i // 2 if q is None else q, i % 2
-        i = 2 * q + b
+            device_id=(origin(chunk, i // 2, i % 2), tp), device_id_type=MESH,
+        )
+
+    def back(chunk, b, k):
+        q = (k + b) % 4 if isinstance(k, int) else lax.rem(k + b, 4)
         return pltpu.make_async_remote_copy(
-            src_ref=x_send.at[chunk, i], dst_ref=r_recv.at[chunk, 2 * q + core],
-            send_sem=rts_sem.at[chunk, i], recv_sem=rtr_sem.at[chunk, 2 * q + core],
-            device_id=(peer(chunk, q, 1) + b, tp), device_id_type=MESH,
+            src_ref=x_send.at[chunk, 2 * k + b], dst_ref=r_recv.at[chunk, 2 * q + core],
+            send_sem=rts_sem.at[chunk, 2 * k + b], recv_sem=rtr_sem.at[chunk, 2 * q + core],
+            device_id=(origin(chunk, k, b), tp), device_id_type=MESH,
         )
 
     def back_arrival(chunk, i):
@@ -164,11 +171,15 @@
             device_id=(peer(chunk, i // 2, -1) + i % 2, tp), device_id_type=MESH,
         )
 
-    def remote_only(chunk, i, act_on):
-        if i < 2:
-            pl.when(jnp.logical_or(chunk != 0, core != i))(act_on)
+    self_spot = 7 * core
+
+    def others(chunk, i, own, act_on):
+        if i in own:
+            pl.when(jnp.logical_or(chunk != 0, core != own.index(i)))(act_on)
         else:
             act_on()
+
+    LISTED, HELD = (0, 1), (0, 7)
 
     def build(chunk):
         for i in range(SPOTS):
@@ -188,11 +199,11 @@
 
     def send_rows(chunk):
         for i in range(SPOTS):
-            remote_only(chunk, i, lambda i=i: dispatch(chunk, i).start())
+            others(chunk, i, LISTED, lambda i=i: dispatch(chunk, i).start())
 
     def take_rows(chunk):
         for i in range(SPOTS):
-            remote_only(chunk, i, lambda i=i: arrival(chunk, i).wait_recv())
+            others(chunk, i, HELD, lambda i=i: arrival(chunk, i).wait_recv())
         for pair in range(SPOTS // 2):
             first = x_recv[chunk, 2 * pair].astype(F32)
             second = x_recv[chunk, 2 * pair + 1].astype(F32)
@@ -322,14 +333,15 @@
         )
         return outs, grads
 
-    def finish_pair(q):
+    def pair_rows(q, e):
+        start = e * exp_rows + (CHUNKS - 1) * half_rows + q * block
+        out = pl.ds(pl.multiple_of(e * block, 16), block)
+        outs, grads = rows_out(e, pl.ds(pl.multiple_of(start, 16), block))
+        fin[out, 0:width] = outs
+        fin[out, width : 2 * width] = grads
+
+    def send_pair(q):
         chunk = CHUNKS - 1
-        for e in range(2):
-            start = e * exp_rows + chunk * half_rows + q * block
-            out = pl.ds(e * block, block)
-            outs, grads = rows_out(e, pl.ds(pl.multiple_of(start, 16), block))
-            fin[out, 0:width] = outs
-            fin[out, width : 2 * width] = grads
         for b in range(2):
             at = b * cap
             both = jnp.concatenate([fin[at : at + cap, :], fin[block + at : block + at + cap, :]], axis=0)
@@ -340,7 +352,7 @@
         ag_last(chunk, 0)
         ag_last(chunk, 1)
         for i in range(SPOTS):
-            remote_only(chunk, i, lambda i=i: dispatch(chunk, i).wait_send())
+            others(chunk, i, LISTED, lambda i=i: dispatch(chunk, i).wait_send())
         for e in range(2):
             span = pl.ds(pl.multiple_of(e * exp_rows + chunk * half_rows, 16), half_rows)
             out = pl.ds(e * half_rows, half_rows)
@@ -356,12 +368,12 @@
                 axis=0,
             )
             x_send[chunk, i] = both.astype(BF)
-            remote_only(chunk, i, lambda i=i: back(chunk, i).start())
+            others(chunk, i, HELD, lambda i=i: back(chunk, i % 2, i // 2).start())
 
     build(0)
     pl.semaphore_wait(barrier, n_ctx + 1)
     send_rows(0)
-    x_recv[0, core] = x_send[0, core]
+    x_recv[0, self_spot] = x_send[0, core]
     build(1)
     for load in loads[2:]:
         load.wait()
@@ -425,40 +437,50 @@
 
     def combine(chunk):
         for i in range(SPOTS):
-            remote_only(chunk, i, lambda: back_arrival(chunk, i).wait_recv())
+            others(chunk, i, LISTED, lambda: back_arrival(chunk, i).wait_recv())
         came = r_recv[chunk, :, :, 0:width].reshape(SPOTS * block, width)
         outs = dot(gate_hi[chunk], came, 0, 0) + dot(gate_lo[chunk], came, 0, 0)
         came = r_recv[chunk, :, :, width : 2 * width].reshape(SPOTS * block, width)
         grads = dot(pick_c[chunk], came, 0, 0)
         if chunk > 0:
-            outs, grads = fin[0:tok, 0:width] + outs, fin[0:tok, width : 2 * width] + grads
+            outs, grads = acc[:, 0:width] + outs, acc[:, width : 2 * width] + grads
+        if chunk < CHUNKS - 1:
+            acc[:, 0:width] = outs
+            acc[:, width : 2 * width] = grads
         return outs, grads
 
     last = CHUNKS - 1
     for i in range(SPOTS):
         dispatch(last, i).wait_send()
+    def finish_pair(q):
+        pair_rows(q, 0)
+        pair_rows(q, 1)
+        send_pair(q)
+
     for step in range(4):
         ag_step(last, 0, step)
         ag_step(last, 1, step)
         if step == 0:
             finish(last - 1)
+            r_recv[0, core] = x_send[0, self_spot]
+        if step == 1:
+            combine(0)
+            combine(1)
         if step == 2:
             finish_pair(lax.rem(tp + 2, 4))
     finish_pair(lax.rem(tp + 1, 4))
     finish_pair(lax.rem(tp + 3, 4))
+    pair_rows(lax.rem(tp, 4), tp // 4)
     ag_last(last, 0)
     ag_last(last, 1)
-    finish_pair(lax.rem(tp, 4))
+    pair_rows(lax.rem(tp, 4), 1 - tp // 4)
+    send_pair(lax.rem(tp, 4))
     for t in range(2):
         for e in range(2):
             weight_grads(t, e)
 
-    r_recv[0, core] = x_send[0, core]
-    for chunk in range(CHUNKS):
-        outs, grads = combine(chunk)
-        if chunk < last:
-            fin[0:tok, 0:width] = outs
-            fin[0:tok, width : 2 * width] = grads
+    combine(2)
+    outs, grads = combine(3)
     moe_out[...] = outs.astype(BF)
     tokens_grad[...] = grads.astype(BF)
 
@@ -468,7 +490,7 @@
                 for step in range(4):
                     ag_copy(chunk, t, way, step).wait_send()
         for i in range(SPOTS):
-            remote_only(chunk, i, lambda i=i, chunk=chunk: back(chunk, i).wait_send())
+            others(chunk, i, HELD, lambda i=i, chunk=chunk: back(chunk, i % 2, i // 2).wait_send())
     for chunk in range(CHUNKS - 2, CHUNKS):
         for t in range(2):
             rs_drain(chunk, t)
@@ -540,6 +562,7 @@
             pltpu.VMEM((CHUNKS, 2, 2, 4, block, wide), BF),
             pltpu.VMEM((2, all_rows, wide), BF),
             pltpu.VMEM((chunk_rows, 2 * width), F32),
+            pltpu.VMEM((tok, 2 * width), F32),
             pltpu.VMEM((CHUNKS, SPOTS, block, 2 * width), BF),
             pltpu.VMEM(w_gu.shape, BF),
             pltpu.VMEM(w_dn.shape, BF),

time: 177 us -> 176 us (level)
  no operation moved by 1% of the time
where the time goes in v4:
time: 176 us; the launch traced here: 175 us
  Pallas kernels  175 us (99%)
    pallas_call x1, Pallas kernels, body(): pl.pallas_call(kernel, out_shape=(jax.ShapeDtypeStruct((tok, width), BF),...  171 us
    pallas_call x1, Pallas kernels, body(): pl.pallas_call(hand_on, out_shape=tuple((jax.ShapeDtypeStruct(r.shape, r....  3.89 us

profile of v4, /device:TPU:1, one launch (start us, length us, event | category | flops | bytes accessed | tf_op | source)
XLA Modules:
  0.0 175.4 jit_solution(3748439103977689373)
XLA Ops:
  0.6 170.8 %moe.1 = (bf16[128,512]{1,0:T(8,128)(2,1)}, bf16[128,512]{1,0:T(8,128)(2,1)}, bf16[2,512,1536]{2,1,0:T(8,128)(2,1)}, bf16[2,768,512]{2,1,0:T(8,128)(2,1)}) custom-call(bf16[128,512]{1,0:T(8,128)(2,1)} %tokens.1, bf16[128,512]{1,0:T(8,128)(2,1)} %out_grad.1, s32[8,128]{1,0:T(8,128)} %bitcast.2, f32[8,128]{1,0:T(8,128)} %bitcast.3, ...), custom_call_target="tpu_custom_call" | custom-call | flops 10871635968 | bytes 10485760 | tf_op jit(solution)/shard_map/moe/pallas_call | solution.py:536
  171.4 3.9 %hand_on.1 = (bf16[128,512]{1,0:T(8,128)(2,1)}, bf16[128,512]{1,0:T(8,128)(2,1)}, bf16[2,512,1536]{2,1,0:T(8,128)(2,1)}, bf16[2,768,512]{2,1,0:T(8,128)(2,1)}) custom-call(bf16[128,512]{1,0:T(8,128)(2,1)} %get-tuple-element.8.refs_0_, bf16[128,512]{1,0:T(8,128)(2,1)} %get-tuple-element.9.refs_1_, bf16[2,512,1536]{2,1,0:T(8,128)(2,1)} %get-tuple-element.10.refs_2_, ...), custom_call_target="tpu_custom_call" | custom-call | tf_op jit(solution)/shard_map/hand_on/pallas_call | solution.py:586

commit v5 on v4

--- a/solution.py
+++ b/solution.py
@@ -18,9 +18,9 @@
 
 OFFSETS = (
     ((0, 0), (1, 0), (3, 0), (0, 1)),
-    ((2, 0), (0, 2), (2, 2), (3, 3)),
-    ((2, 1), (2, 3), (1, 2), (3, 2)),
-    ((0, 3), (1, 1), (3, 1), (1, 3)),
+    ((2, 2), (2, 1), (2, 3), (1, 2)),
+    ((2, 0), (0, 2), (3, 2), (1, 3)),
+    ((0, 3), (1, 1), (3, 3), (3, 1)),
 )
 
 
@@ -39,7 +39,7 @@
     tokens, out_grad, routes_in, gates_in, w_gu, w_dn,
     moe_out, tokens_grad, wgu_out, wdn_out,
     routes, gates, tg, pick_all, gate_all, pick_c, gate_hi, gate_lo,
-    x_send, x_recv, rows, wgu, wdn, part, rs_send, rs_recv, act, fin, acc, r_recv, wgu_st, wdn_st,
+    x_send, x_recv, rows, wgu, wdn, part, rs_send, rs_recv, act, fin, acc, r_recv, wgu_st, wdn_st, gu_sum, dn_sum,
     ld_sem, xs_sem, xr_sem, rss_sem, rsr_sem, ags_sem, agr_sem, rts_sem, rtr_sem, out_sem,
 ):
     ctx = lax.axis_index("ctx")
@@ -419,20 +419,28 @@
         stores.append(pltpu.make_async_copy(src, dst, out_sem.at[len(stores)]))
         stores[-1].start()
 
+    def grad_terms(t, e, first, count):
+        span = slice(e * exp_rows + first, e * exp_rows + first + count)
+        gu = dot(rows[span, 0:width], act[t, span, strip:wide], 0, 0)
+        dn = dot(act[t, span, 0:strip], rows[span, width : 2 * width], 0, 0)
+        return gu, dn
+
+    ready = (CHUNKS - 1) * half_rows
+
+    def most_grads(t, e):
+        gu, dn = grad_terms(t, e, 0, ready)
+        gu_sum[t, e], dn_sum[t, e] = gu, dn
+
     def weight_grads(t, e):
-        span = slice(e * exp_rows, (e + 1) * exp_rows)
-        wgu_st[e, :, t * ff : (t + 1) * ff] = dot(
-            rows[span, 0:width], act[t, span, strip:wide], 0, 0
-        ).astype(BF)
+        gu, dn = grad_terms(t, e, ready, exp_rows - ready)
+        wgu_st[e, :, t * ff : (t + 1) * ff] = (gu_sum[t, e] + gu).astype(BF)
         for u in range(2):
             store(
                 wgu_st.at[e, :, pl.ds(t * ff + u * strip, strip)],
                 wgu_out.at[e, :, pl.ds(u * ff + t * strip, strip)],
             )
-        wdn_st[e, t * strip : (t + 1) * strip, :] = dot(
-            act[t, span, 0:strip], rows[span, width : 2 * width], 0, 0
-        ).astype(BF)
         at = pl.ds(t * strip, strip)
+        wdn_st[e, at, :] = (dn_sum[t, e] + dn).astype(BF)
         store(wdn_st.at[e, at], wdn_out.at[e, at])
 
     def combine(chunk):
@@ -466,8 +474,12 @@
         if step == 1:
             combine(0)
             combine(1)
+            most_grads(0, 0)
+            most_grads(0, 1)
         if step == 2:
             finish_pair(lax.rem(tp + 2, 4))
+            most_grads(1, 0)
+            most_grads(1, 1)
     finish_pair(lax.rem(tp + 1, 4))
     finish_pair(lax.rem(tp + 3, 4))
     pair_rows(lax.rem(tp, 4), tp // 4)
@@ -566,6 +578,8 @@
             pltpu.VMEM((CHUNKS, SPOTS, block, 2 * width), BF),
             pltpu.VMEM(w_gu.shape, BF),
             pltpu.VMEM(w_dn.shape, BF),
+            pltpu.VMEM((2, 2, width, ff), F32),
+            pltpu.VMEM((2, 2, ff // 2, width), F32),
             dma((9,)),
             dma((CHUNKS, SPOTS)),
             dma((CHUNKS, SPOTS)),

time: 176 us -> 175 us (level)
  no operation moved by 1% of the time
where the time goes in v5:
time: 175 us
  Pallas kernels  174 us (99%)
    pallas_call x1, Pallas kernels, body(): pl.pallas_call(kernel, out_shape=(jax.ShapeDtypeStruct((tok, width), BF),...  170 us
    pallas_call x1, Pallas kernels, body(): pl.pallas_call(hand_on, out_shape=tuple((jax.ShapeDtypeStruct(r.shape, r....  3.89 us

profile of v5, /device:TPU:1, one launch (start us, length us, event | category | flops | bytes accessed | tf_op | source)
XLA Modules:
  0.0 175.1 jit_solution(8819454357675161653)
XLA Ops:
  0.6 170.4 %moe.1 = (bf16[128,512]{1,0:T(8,128)(2,1)}, bf16[128,512]{1,0:T(8,128)(2,1)}, bf16[2,512,1536]{2,1,0:T(8,128)(2,1)}, bf16[2,768,512]{2,1,0:T(8,128)(2,1)}) custom-call(bf16[128,512]{1,0:T(8,128)(2,1)} %tokens.1, bf16[128,512]{1,0:T(8,128)(2,1)} %out_grad.1, s32[8,128]{1,0:T(8,128)} %bitcast.2, f32[8,128]{1,0:T(8,128)} %bitcast.3, ...), custom_call_target="tpu_custom_call" | custom-call | flops 10871635968 | bytes 10485760 | tf_op jit(solution)/shard_map/moe/pallas_call | solution.py:548
  171.0 3.9 %hand_on.1 = (bf16[128,512]{1,0:T(8,128)(2,1)}, bf16[128,512]{1,0:T(8,128)(2,1)}, bf16[2,512,1536]{2,1,0:T(8,128)(2,1)}, bf16[2,768,512]{2,1,0:T(8,128)(2,1)}) custom-call(bf16[128,512]{1,0:T(8,128)(2,1)} %get-tuple-element.8.refs_0_, bf16[128,512]{1,0:T(8,128)(2,1)} %get-tuple-element.9.refs_1_, bf16[2,512,1536]{2,1,0:T(8,128)(2,1)} %get-tuple-element.10.refs_2_, ...), custom_call_target="tpu_custom_call" | custom-call | tf_op jit(solution)/shard_map/hand_on/pallas_call | solution.py:600
